TPU v7x, 32 devices: a whole 2x2x4 slice. The times are simulated.
32 devices in a mesh: index: 4 (over y, core), bulk: 8 (over z, x).
Axes of the slice: x: 2, y: 2, z: 4, core: 2. Of those that a mesh axis runs over, the one named last changes fastest.
Arguments:
- questions: bfloat16 [1024, 768], P(('index', 'bulk')), may hold values from -26 to 26
- passages: bfloat16 [65536, 768], P(('index', 'bulk')), may hold values from -6 to 6
- candidate_ids: int32 [1024, 32], P(('index', 'bulk')), may hold values from 0 to 65535, as said below
- reader_loglik: float32 [1024, 32], P(('index', 'bulk')), may hold values from -400 to 0
Outputs:
- mean_divergence: float32 [], replicated
- question_grads: float32 [1024, 768], P(('index', 'bulk'))
Inputs may be any that keep to these rules, and one draw needn't show every extreme that they name: `candidate_ids`: passage id p lies in the range of owner p // 2048. Among the 32 candidates of the 32 questions of one device, at most 64 lie in one owner's range; in every draw some owner has exactly 64 from every device, and every owner has at least one from every device.
All inputs are finite; a program needn't handle non-finite values.
Results may differ from a plain program's by a relative error of at most 0.0024.
Values may be sent and summed in bfloat16 or wider, within the bound.
A program may use at most 64 MiB of HBM per device.

v0:
```python
import math

import jax
import jax.numpy as jnp
from jax import lax
from jax.sharding import PartitionSpec as P


def log_normalize(logits):
    highest = jnp.max(logits, axis=1, keepdims=True)
    shifted = logits - highest
    return shifted - jnp.log(jnp.sum(jnp.exp(shifted), axis=1, keepdims=True))


def send_requests(request):
    return lax.all_to_all(request, ("index", "bulk"), split_axis=0, concat_axis=0, tiled=True)


def return_rows(fetched):
    return lax.all_to_all(fetched, ("index", "bulk"), split_axis=0, concat_axis=0, tiled=True)


def body(questions, passages, candidate_ids, reader_loglik):
    owners = lax.axis_size(("index", "bulk"))
    question_count, candidates = candidate_ids.shape
    per_owner, feature_width = passages.shape
    pair_count = question_count * candidates
    capacity = 2 * pair_count // owners
    flat_ids = candidate_ids.reshape(pair_count)
    owner_of = flat_ids // per_owner
    row_of = flat_ids % per_owner
    member = (owner_of[:, None] == jnp.arange(owners, dtype=jnp.int32)[None, :]).astype(jnp.int32)
    earlier = jnp.cumsum(member, axis=0) - member
    send_slot = owner_of * capacity + jnp.sum(earlier * member, axis=1)
    request = jnp.zeros((owners * capacity,), jnp.int32).at[send_slot].set(row_of)
    log_reader = log_normalize(reader_loglik)
    reader_prob = jnp.exp(log_reader)
    wanted = send_requests(request)
    fetched = jnp.take(passages, wanted, axis=0)
    replies = return_rows(fetched)
    gathered = jnp.take(replies, send_slot, axis=0).reshape(
        question_count, candidates, feature_width
    )
    score_scale = 4.0 / math.sqrt(feature_width)
    scores = (
        jnp.einsum("qd,qkd->qk", questions, gathered, preferred_element_type=jnp.float32)
        * score_scale
    )
    log_retriever = log_normalize(scores)
    retriever_prob = jnp.exp(log_retriever)
    divergence = jnp.sum(reader_prob * (log_reader - log_retriever), axis=1)
    summed = lax.psum(jnp.sum(divergence), ("index", "bulk"))
    mean_divergence = summed / (question_count * owners)
    weights = (retriever_prob - reader_prob).astype(jnp.bfloat16)
    question_grads = (
        jnp.einsum("qk,qkd->qd", weights, gathered, preferred_element_type=jnp.float32)
        * score_scale
    )
    return (mean_divergence, question_grads)


def solution(mesh):
    placed = (
        P(("index", "bulk"), None),
        P(("index", "bulk"), None),
        P(("index", "bulk"), None),
        P(("index", "bulk"), None),
    )
    return jax.shard_map(
        body,
        mesh=mesh,
        in_specs=placed,
        out_specs=(P(), P(("index", "bulk"), None)),
        check_vma=False,
    )
```

profile of v0, /device:TPU:0, one launch (start us, length us, event | category | flops | bytes accessed | tf_op | source)
XLA Modules:
  0.0 172.7 jit_solution(8512238889316238467)
XLA Ops:
  0.6 0.9 reshape.198
  1.6 0.8 reshape.197
  2.4 0.8 reshape.200
  3.2 9.0 %reduce-window.6 = s32[32,8,128]{2,1,0:T(8,128)S(1)} reduce-window(s32[32,8,128]{2,1,0:T(8,128)S(1)} %fusion.7, s32[]{:T(128)} %constant.64.clone.1), window={size=1x1x128 pad=0_0x0_0x127_0}, to_apply=%region_2.3 | reduce-window | flops 4161536 | bytes 262148 | tf_op jit(solution)/shard_map/reduce-window
  12.3 0.1 copy.8
  12.6 0.1 broadcast_add_fusion
  12.8 4.3 %scatter_custom_fusion = s32[2048]{0:T(1024)S(1)} fusion(s32[1024]{0:T(1024)S(1)} %bitcast.44, s32[1024]{0:T(1024)S(1)} %get-tuple-element.4, s32[]{:T(128)} %constant.64.clone.1), kind=kCustom, calls=%fused_computation.57 | custom fusion | bytes 8196 | tf_op jit(solution)/shard_map/scatter | solution.py:35
  17.2 14.2 %all_to_all.24 = s32[32,64,1]{1,2,0:T(1,128)S(1)} all-to-all(s32[32,64,1]{1,2,0:T(1,128)S(1)} %all_to_all.16), channel_id=1, replica_groups=mesh['index'=4,'bulk'=8] {'index','bulk'}, dimensions={0} | all-to-all | bytes 16384 | tf_op jit(solution)/shard_map/all_to_all | solution.py:16
  31.4 0.5 broadcast.219
  31.9 0.7 reduce.4
  32.7 9.4 %gather_fusion = bf16[2048,768]{1,0:T(8,128)(2,1)} fusion(bf16[2048,768]{1,0:T(8,128)(2,1)S(1)} %copy-done, s32[2048]{0:T(1024)S(1)} %broadcast_clamp_fusion), kind=kCustom, calls=%fused_computation | custom fusion | bytes 6299648 | tf_op jit(solution)/shard_map/jit(_take)/gather | solution.py:39
  42.1 3.3 %broadcast_select_fusion = bf16[32,64,768]{2,1,0:T(8,128)(2,1)} fusion(bf16[32,64,768]{2,1,0:T(8,128)(2,1)} %bitcast.33, pred[32,64]{1,0:T(8,128)(4,1)S(1)} %compare_and_fusion), kind=kLoop, calls=%fused_computation.3 | loop fusion | flops 1572864 | bytes 6293504 | tf_op jit(solution)/shard_map/jit(_take)/select_n | solution.py:39
  45.5 3.7 %all-to-all-start.1 = ((bf16[32,64,768]{2,1,0:T(8,128)(2,1)}), bf16[32,64,768]{2,1,0:T(8,128)(2,1)}, u32[]{:S(2)}, u32[]{:S(2)}) async-start(bf16[32,64,768]{2,1,0:T(8,128)(2,1)} %broadcast_select_fusion), calls=%async_computation.1 | async-start | bytes 6291456 | tf_op jit(solution)/shard_map/all_to_all | solution.py:20
  49.2 0.1 reduce_max.18
  49.3 0.2 exponential_reduce_fusion.1
  49.6 72.2 %all-to-all-done.1 = bf16[32,64,768]{2,1,0:T(8,128)(2,1)} async-done(((bf16[32,64,768]{2,1,0:T(8,128)(2,1)}), bf16[32,64,768]{2,1,0:T(8,128)(2,1)}, u32[]{:S(2)}, u32[]{:S(2)}) %all-to-all-start.1) | async-done | bytes 3145760 | tf_op jit(solution)/shard_map/all_to_all | solution.py:20
  121.8 7.9 %gather_fusion.1 = bf16[1024,768]{1,0:T(8,128)(2,1)} fusion(bf16[2048,768]{1,0:T(8,128)(2,1)} %bitcast.7, s32[1024]{0:T(1024)S(1)} %broadcast_clamp_fusion.1), kind=kCustom, calls=%fused_computation.1 | custom fusion | bytes 3149824 | tf_op jit(solution)/shard_map/jit(_take)/gather | solution.py:41
  129.6 2.1 %fusion.1 = f32[32,1,32]{2,1,0:T(1,128)S(1)} fusion(bf16[32,32,768]{2,1,0:T(8,128)(2,1)} %bitcast.34, pred[32,32]{1,0:T(8,128)(4,1)S(1)} %compare_and_fusion.1, bf16[32,768,1]{1,0,2:T(8,128)(2,1)S(1)} %bitcast.46), kind=kOutput, calls=%fused_computation.6 | convolution fusion | flops 2359296 | bytes 1627136 | tf_op jit(solution)/shard_map/qd,qkd->qk/dot_general | solution.py:46
  131.7 0.1 multiply_reduce_fusion.1
  131.9 0.2 exponential_reduce_fusion
  132.1 0.7 fusion.14
  132.8 0.4 fusion
  133.2 0.7 bitcast_multiply_fusion
  133.8 37.1 %psum.7 = f32[]{:T(128)} all-reduce(f32[]{:T(128)} %get-tuple-element.3), channel_id=1, replica_groups=mesh['index'=4,'bulk'=8] {'index','bulk'}, use_global_device_ids=true, to_apply=%region_9.10 | all-reduce | flops 1 | bytes 8 | tf_op jit(solution)/shard_map/psum | solution.py:52
  (29 shorter events, 0.6 us)
Async XLA Ops:
  0.6 32.1 %copy-start = (bf16[2048,768]{1,0:T(8,128)(2,1)S(1)}, bf16[2048,768]{1,0:T(8,128)(2,1)}, u32[]{:S(2)}) copy-start(bf16[2048,768]{1,0:T(8,128)(2,1)} %param.5) | copy-start | bytes 9437188
  45.5 3.7 %copy-start.3 = (f32[32,32]{1,0:T(8,128)S(1)}, f32[32,32]{1,0:T(8,128)}, u32[]{:S(2)}) copy-start(f32[32,32]{1,0:T(8,128)} %param.7) | copy-start | bytes 12292
  45.5 4.1 %copy-start.2 = (s32[32,32]{1,0:T(8,128)S(1)}, s32[32,32]{1,0:T(8,128)}, u32[]{:S(2)}) copy-start(s32[32,32]{1,0:T(8,128)} %param.6) | copy-start | bytes 12292
  45.5 76.3 %all-to-all-start.1 = ((bf16[32,64,768]{2,1,0:T(8,128)(2,1)}), bf16[32,64,768]{2,1,0:T(8,128)(2,1)}, u32[]{:S(2)}, u32[]{:S(2)}) async-start(bf16[32,64,768]{2,1,0:T(8,128)(2,1)} %broadcast_select_fusion), calls=%async_computation.1 | async-start | bytes 6291456 | tf_op jit(solution)/shard_map/all_to_all | solution.py:20
  121.8 7.9 %copy-start.4 = (bf16[32,768]{1,0:T(8,128)(2,1)S(1)}, bf16[32,768]{1,0:T(8,128)(2,1)}, u32[]{:S(2)}) copy-start(bf16[32,768]{1,0:T(8,128)(2,1)} %param.4) | copy-start | bytes 147460
  129.6 3.1 %copy-start.1 = (bf16[1024,768]{1,0:T(8,128)(2,1)S(1)}, bf16[1024,768]{1,0:T(8,128)(2,1)}, u32[]{:S(2)}) copy-start(bf16[1024,768]{1,0:T(8,128)(2,1)} %gather_fusion.1) | copy-start | bytes 4718596
where the time goes:
time: 174 us; the launch traced here: 173 us
  waiting for transfers between devices  72.2 us (41%)
  blocking collectives  51.3 us (29%)
  local copies, waits for them, and re-layouts  25.2 us (14%)
  other arithmetic  15.3 us (9%)
  starting transfers between devices  3.65 us (2%)
  between operations  2.59 us (1%)
  matrix products  2.5 us (1%)
    all_to_all x1, waiting for transfers between devices, return_rows(): lax.all_to_all(fetched, ('index', 'bulk'), split_axis=0, concat_axis=0, t...  72.2 us
    psum x1, blocking collectives, body(): summed = lax.psum(jnp.sum(divergence), ('index', 'bulk'))  37.1 us
    all_to_all x1, blocking collectives, send_requests(): lax.all_to_all(request, ('index', 'bulk'), split_axis=0, concat_axis=0, t...  14.2 us
    gather x1, local copies, waits for them, and re-layouts, body(): fetched = jnp.take(passages, wanted, axis=0)  9.38 us
    another operation x3, other arithmetic  9.15 us
    gather x1, local copies, waits for them, and re-layouts, body(): jnp.take(replies, send_slot, axis=0)  7.86 us
    scatter x1, local copies, waits for them, and re-layouts, body(): jnp.zeros((owners * capacity,), jnp.int32).at[send_slot].set(row_of)  4.32 us
    all_to_all x1, starting transfers between devices, return_rows(): lax.all_to_all(fetched, ('index', 'bulk'), split_axis=0, concat_axis=0, t...  3.65 us
  transfers between devices with their start and end apart: 1, of which 1 were waited for; matrix products, arithmetic and copies ran while one was open for 0% of the time, Pallas kernels for 0%

commit v1 on v0

v1 whole, which is shorter than its diff:
```python
import functools
import math

import jax
import jax.numpy as jnp
from jax import lax
from jax.experimental import pallas as pl
from jax.experimental.pallas import tpu as pltpu
from jax.sharding import PartitionSpec as P

MESH = pl.DeviceIdType.MESH
LANES = 128
VMEM_LIMIT = 56 * 1024 * 1024


class Place:
    def __init__(self, sizes):
        self.ny, self.nz, self.nx = sizes
        self.nb = self.nz * self.nx
        self.n = self.ny * 2 * self.nb
        index, bulk = lax.axis_index("index"), lax.axis_index("bulk")
        self.y, self.c = index // 2, index % 2
        self.z, self.x = bulk // self.nx, bulk % self.nx
        self.me = index * self.nb + bulk

    def number(self, y, c, z, x):
        return (y * 2 + c) * self.nb + z * self.nx + x

    def device(self, y, c, z, x):
        return (y * 2 + c, z * self.nx + x)

    def device_of(self, number):
        return (number // self.nb, number % self.nb)

    def plane(self):
        for a in range(self.ny):
            for b in range(self.nx):
                if a or b:
                    yield (a * self.nx + b, (self.y + a) % self.ny, (self.x + b) % self.nx)


def greet_all(place):
    barrier = pltpu.get_barrier_semaphore()

    def greet(i, carry):
        pl.semaphore_signal(
            barrier, inc=1, device_id=place.device_of((place.me + i) % place.n), device_id_type=MESH
        )
        return carry

    lax.fori_loop(1, place.n, greet, 0)
    pl.semaphore_wait(barrier, place.n - 1)


def to_all(place, src_of, dst, send_sem, recv_sem):
    def send(i, carry):
        other = (place.me + i) % place.n
        pltpu.make_async_remote_copy(
            src_ref=src_of(other), dst_ref=dst, send_sem=send_sem, recv_sem=recv_sem,
            device_id=place.device_of(other), device_id_type=MESH,
        ).start()
        return carry

    lax.fori_loop(1, place.n, send, 0)


def wait_bytes(ref, sem):
    pltpu.make_async_copy(ref, ref, sem).wait()


def gather_kernel(sizes, q_ref, id_ref, qall, idall, send_sem, recv_sem, id_send, id_recv):
    t = Place(sizes)
    rows, id_rows = q_ref.shape[0], id_ref.shape[0]
    greet_all(t)

    def block(number):
        return qall.at[pl.ds(pl.multiple_of(number * rows, rows), rows)]

    def copy(src, number, device):
        return pltpu.make_async_remote_copy(
            src_ref=src, dst_ref=block(number), send_sem=send_sem, recv_sem=recv_sem.at[number],
            device_id=device, device_id_type=MESH,
        )

    def arrived(number):
        wait_bytes(block(number), recv_sem.at[number])

    sibling = t.device(t.y, 1 - t.c, t.z, t.x)
    for i in range(1, t.nz):
        copy(q_ref, t.me, t.device(t.y, t.c, (t.z + i) % t.nz, t.x)).start()
    for _, y, x in t.plane():
        copy(q_ref, t.me, t.device(y, t.c, t.z, x)).start()
    copy(q_ref, t.me, sibling).start()
    my_ids = idall.at[pl.ds(pl.multiple_of(t.me * id_rows, id_rows), id_rows)]
    to_all(t, lambda other: id_ref, my_ids, id_send, id_recv)
    qall[pl.ds(pl.multiple_of(t.me * rows, rows), rows), :] = q_ref[...]
    idall[pl.ds(pl.multiple_of(t.me * id_rows, id_rows), id_rows), :] = id_ref[...]
    for i in range(1, t.nz):
        number = t.number(t.y, t.c, (t.z + i) % t.nz, t.x)
        arrived(number)
        for _, y, x in t.plane():
            copy(block(number), number, t.device(y, t.c, t.z, x)).start()
        copy(block(number), number, sibling).start()
    for i in range(t.nz):
        for _, y, x in t.plane():
            number = t.number(y, t.c, (t.z + i) % t.nz, x)
            arrived(number)
            copy(block(number), number, sibling).start()
    for i in range(t.nz):
        arrived(t.number(t.y, 1 - t.c, (t.z + i) % t.nz, t.x))
        for _, y, x in t.plane():
            arrived(t.number(y, 1 - t.c, (t.z + i) % t.nz, x))
    others = qall.at[pl.ds(0, (t.n - 1) * rows)]
    wait_bytes(others, send_sem)
    other_ids = idall.at[pl.ds(0, (t.n - 1) * id_rows)]
    wait_bytes(other_ids, id_recv)
    wait_bytes(other_ids, id_send)


def score_kernel(sizes, chunk, k, qall, p_ref, idall, out, s):
    t = Place(sizes)
    per, width = p_ref.shape
    tiles, group = per // LANES, LANES // k
    id_rows = idall.shape[0] // t.n
    rows = id_rows * group
    lane_group = lax.broadcasted_iota(jnp.int32, (id_rows, LANES), 1) // k

    def one_chunk(g, carry):
        q = qall[pl.ds(pl.multiple_of(g * chunk * rows, chunk * rows), chunk * rows), :]
        for h in range(0, tiles, 2):
            both = lax.dot_general(
                q, p_ref[h * LANES:(h + 2) * LANES, :],
                (((1,), (1,)), ((), ())), preferred_element_type=jnp.float32,
            )
            s[h] = both[:, :LANES]
            s[h + 1] = both[:, LANES:]

        def one_device(i, carry):
            at = pl.ds(pl.multiple_of((g * chunk + i) * id_rows, id_rows), id_rows)
            local = idall[at, :] - t.me * per
            own = (local >= 0) & (local < per)
            code = jnp.where(own, lane_group * tiles + local // LANES, -1)
            low = local & (LANES - 1)
            total = jnp.zeros((id_rows, LANES), jnp.float32)
            for j in range(group):
                for h in range(tiles):
                    piece = s[h, pl.ds(i * rows + j, id_rows, stride=group), :]
                    picked = jnp.take_along_axis(piece, low, axis=1)
                    total = jnp.where(code == j * tiles + h, picked, total)
            out[at, :] = total
            return carry

        return lax.fori_loop(0, chunk, one_device, carry)

    lax.fori_loop(0, t.n // chunk, one_chunk, 0)


def grouped(x, k, reduce, empty):
    group = lax.broadcasted_iota(jnp.int32, x.shape, 1) // k
    result = jnp.full(x.shape, empty, x.dtype)
    for j in range(x.shape[1] // k):
        value = reduce(jnp.where(group == j, x, empty), axis=1, keepdims=True)
        result = jnp.where(group == j, value, result)
    return result


def log_normalize(x, k):
    shifted = x - grouped(x, k, jnp.max, -jnp.inf)
    return shifted - jnp.log(grouped(jnp.exp(shifted), k, jnp.sum, 0.0))


def weight_kernel(sizes, k, scale, ps, reader, wall, mean, srecv, mine, mall,
                  s_send, s_recv, w_send, w_recv):
    t = Place(sizes)
    r = reader.shape[0]
    greet_all(t)

    def rows(number, count):
        return pl.ds(pl.multiple_of(number * count, count), count)

    to_all(t, lambda other: ps.at[rows(other, r)], srecv.at[rows(t.me, r)], s_send, s_recv)
    srecv[rows(t.me, r), :] = ps[rows(t.me, r), :]
    log_reader = log_normalize(reader[...], k)
    reader_prob = jnp.exp(log_reader)
    wait_bytes(srecv.at[pl.ds(0, (t.n - 1) * r)], s_recv)
    scores = jnp.sum(srecv[...].reshape(t.n, r, LANES), axis=0) * scale
    log_retriever = log_normalize(scores, k)
    weights = (jnp.exp(log_retriever) - reader_prob).astype(jnp.bfloat16).astype(jnp.float32)
    mine[0:r, :] = weights
    mine[r:2 * r, :] = reader_prob * (log_reader - log_retriever)
    to_all(t, lambda other: mine, mall.at[rows(t.me, 2 * r)], w_send, w_recv)
    mall[rows(t.me, 2 * r), :] = mine[...]
    wait_bytes(mall.at[pl.ds(0, (t.n - 1) * 2 * r)], w_recv)
    parts = mall[...].reshape(t.n, 2 * r, LANES)
    wall[...] = parts[:, :r, :].reshape(t.n * r, LANES)
    total = jnp.sum(jnp.sum(parts[:, r:, :], axis=0))
    mean[0, 0] = total / (t.n * r * LANES // k)
    wait_bytes(srecv.at[pl.ds(0, (t.n - 1) * r)], s_send)
    wait_bytes(mall.at[pl.ds(0, (t.n - 1) * 2 * r)], w_send)


def grad_kernel(sizes, chunk, k, wall, p_ref, idall, out, wd):
    t = Place(sizes)
    per, width = p_ref.shape
    tiles, group = per // LANES, LANES // k
    id_rows = idall.shape[0] // t.n
    rows = id_rows * group
    pair = 8 // group
    lane_group = lax.broadcasted_iota(jnp.int32, (id_rows, LANES), 1) // k
    row_part = lax.broadcasted_iota(jnp.int32, (id_rows, LANES), 0) % pair
    spot = lax.broadcasted_iota(jnp.int32, (8 * tiles, LANES), 0)
    place_in = lax.broadcasted_iota(jnp.int32, (LANES, LANES), 0)

    def one_chunk(g, carry):
        def one_device(i, carry):
            at = pl.ds(pl.multiple_of((g * chunk + i) * id_rows, id_rows), id_rows)
            local = idall[at, :] - t.me * per
            own = (local >= 0) & (local < per)
            code = jnp.where(own, (local // LANES) * 8 + row_part * group + lane_group, -1)
            low = local & (LANES - 1)
            w = wall[at, :]
            for a in range(0, id_rows, pair):
                left = jnp.concatenate(
                    [jnp.where(spot == code[b:b + 1, :], w[b:b + 1, :], 0.0) for b in range(a, a + pair)],
                    axis=1).astype(jnp.bfloat16)
                right = jnp.concatenate(
                    [jnp.where(place_in == low[b:b + 1, :], 1.0, 0.0) for b in range(a, a + pair)],
                    axis=1).astype(jnp.bfloat16)
                dense = lax.dot_general(
                    left, right, (((1,), (1,)), ((), ())), preferred_element_type=jnp.float32)
                to = pl.ds(pl.multiple_of(i * rows + a * group, 8), 8)
                for h in range(tiles):
                    wd[to, h * LANES:(h + 1) * LANES] = dense[h * 8:(h + 1) * 8, :]
            return carry

        lax.fori_loop(0, chunk, one_device, 0)
        out[pl.ds(pl.multiple_of(g * chunk * rows, chunk * rows), chunk * rows), :] = jnp.dot(
            wd[...].astype(jnp.bfloat16), p_ref[...], preferred_element_type=jnp.float32)
        return carry

    lax.fori_loop(0, t.n // chunk, one_chunk, 0)


def reduce_kernel(sizes, scale, g_ref, out, sib, acc, going, coming, zin,
                  sib_send, sib_recv, p_send, p_recv, z_send, z_recv):
    t = Place(sizes)
    rows = out.shape[0]
    greet_all(t)

    def span(number, count=1):
        return pl.ds(pl.multiple_of(number * rows, rows), count * rows)

    order = list(range(1, t.nz)) + [0]
    firsts = []
    for i in order:
        z = (t.z + i) % t.nz
        for y in range(t.ny):
            slot = i * t.ny + y
            copy = pltpu.make_async_remote_copy(
                src_ref=g_ref.at[span(t.number(y, 1 - t.c, z, 0), t.nx)],
                dst_ref=sib.at[span(y * t.nb + z * t.nx, t.nx)],
                send_sem=sib_send.at[slot], recv_sem=sib_recv.at[slot],
                device_id=t.device(t.y, 1 - t.c, t.z, t.x), device_id_type=MESH,
            )
            copy.start()
            firsts.append(copy)
    at = 0
    seconds = {}
    for i in order:
        z = (t.z + i) % t.nz
        for y in range(t.ny):
            firsts[at].wait_recv()
            at += 1

        def summed(y, x):
            return g_ref[span(t.number(y, t.c, z, x)), :] + sib[span(y * t.nb + z * t.nx + x), :]

        for o, y, x in t.plane():
            going[i, o] = summed(y, x).astype(jnp.bfloat16)
            copy = pltpu.make_async_remote_copy(
                src_ref=going.at[i, o], dst_ref=coming.at[i, o],
                send_sem=p_send.at[i, o], recv_sem=p_recv.at[i, o],
                device_id=t.device(y, t.c, t.z, x), device_id_type=MESH,
            )
            copy.start()
            seconds[i, o] = copy
        acc[i] = summed(t.y, t.x)
    thirds = []
    for i in order:
        total = acc[i]
        for o, _, _ in t.plane():
            seconds[i, o].wait_recv()
            total = total + coming[i, o].astype(jnp.float32)
        acc[i] = total
        if i:
            copy = pltpu.make_async_remote_copy(
                src_ref=acc.at[i], dst_ref=zin.at[i],
                send_sem=z_send.at[i], recv_sem=z_recv.at[i],
                device_id=t.device(t.y, t.c, (t.z + i) % t.nz, t.x), device_id_type=MESH,
            )
            copy.start()
            thirds.append((i, copy))
    total = acc[0]
    for i, copy in thirds:
        copy.wait_recv()
        total = total + zin[i]
    out[...] = total * scale
    for copy in firsts + list(seconds.values()) + [copy for _, copy in thirds]:
        copy.wait_send()


def solution(mesh):
    n_index, n_bulk = mesh.shape["index"], mesh.shape["bulk"]
    ny = n_index // 2
    nx = math.gcd(ny, n_bulk)
    sizes = (ny, n_bulk // nx, nx)
    nz = sizes[1]
    n = n_index * n_bulk
    vmem = pl.BlockSpec(memory_space=pltpu.VMEM)
    dma = pltpu.SemaphoreType.DMA

    def remote(number):
        return pltpu.CompilerParams(
            collective_id=number, has_side_effects=True, vmem_limit_bytes=VMEM_LIMIT)

    local = pltpu.CompilerParams(vmem_limit_bytes=VMEM_LIMIT)

    def body(questions, passages, candidate_ids, reader_loglik):
        rows, k = candidate_ids.shape
        width = passages.shape[1]
        per = passages.shape[0]
        id_rows = rows * k // LANES
        scale = 4.0 / math.sqrt(width)
        ids = candidate_ids.reshape(id_rows, LANES)
        reader = reader_loglik.reshape(id_rows, LANES)
        chunk = 8
        f32, bf16, i32 = jnp.float32, jnp.bfloat16, jnp.int32

        qall, idall = pl.pallas_call(
            functools.partial(gather_kernel, sizes),
            out_shape=(jax.ShapeDtypeStruct((n * rows, width), bf16),
                       jax.ShapeDtypeStruct((n * id_rows, LANES), i32)),
            in_specs=[vmem] * 2, out_specs=(vmem, vmem),
            scratch_shapes=[dma, dma((n,)), dma, dma],
            compiler_params=remote(0), name="gather_questions",
        )(questions, ids)
        partial = pl.pallas_call(
            functools.partial(score_kernel, sizes, chunk, k),
            out_shape=jax.ShapeDtypeStruct((n * id_rows, LANES), f32),
            in_specs=[vmem] * 3, out_specs=vmem,
            scratch_shapes=[pltpu.VMEM((per // LANES, chunk * rows, LANES), f32)],
            compiler_params=local, name="owner_scores",
        )(qall, passages, idall)
        wall, mean = pl.pallas_call(
            functools.partial(weight_kernel, sizes, k, scale),
            out_shape=(jax.ShapeDtypeStruct((n * id_rows, LANES), f32),
                       jax.ShapeDtypeStruct((1, 1), f32)),
            in_specs=[vmem] * 2, out_specs=(vmem, pl.BlockSpec(memory_space=pltpu.SMEM)),
            scratch_shapes=[pltpu.VMEM((n * id_rows, LANES), f32),
                            pltpu.VMEM((2 * id_rows, LANES), f32),
                            pltpu.VMEM((n * 2 * id_rows, LANES), f32),
                            dma, dma, dma, dma],
            compiler_params=remote(1), name="exchange_weights",
        )(partial, reader)
        grads = pl.pallas_call(
            functools.partial(grad_kernel, sizes, chunk, k),
            out_shape=jax.ShapeDtypeStruct((n * rows, width), f32),
            in_specs=[vmem] * 3, out_specs=vmem,
            scratch_shapes=[pltpu.VMEM((chunk * rows, per), f32)],
            compiler_params=local, name="owner_grads",
        )(wall, passages, idall)
        flat = ny * nx
        question_grads = pl.pallas_call(
            functools.partial(reduce_kernel, sizes, scale),
            out_shape=jax.ShapeDtypeStruct((rows, width), f32),
            in_specs=[vmem], out_specs=vmem,
            scratch_shapes=[pltpu.VMEM((n // 2 * rows, width), f32),
                            pltpu.VMEM((nz, rows, width), f32),
                            pltpu.VMEM((nz, flat, rows, width), bf16),
                            pltpu.VMEM((nz, flat, rows, width), bf16),
                            pltpu.VMEM((nz, rows, width), f32),
                            dma((nz * ny,)), dma((nz * ny,)),
                            dma((nz, flat)), dma((nz, flat)), dma((nz,)), dma((nz,))],
            compiler_params=remote(2), name="reduce_grads",
        )(grads)
        return mean[0, 0], question_grads

    placed = P(("index", "bulk"), None)
    return jax.shard_map(
        body, mesh=mesh, in_specs=(placed,) * 4, out_specs=(P(), placed), check_vma=False)
```

time: 174 us -> 98.8 us (0.57)
  Pallas kernels: 0 us -> 91.6 us
  waiting for transfers between devices: 72.2 us -> 0 us
  blocking collectives: 51.3 us -> 0 us
  local copies, waits for them, and re-layouts: 25.2 us -> 4.3 us
  other arithmetic: 15.3 us -> 0 us
  starting transfers between devices: 3.65 us -> 0 us
  matrix products: 2.5 us -> 0 us
    pallas_call x0 -> x5, Pallas kernels: none -> 91.6 us  [the longest x1 22.7 us: body(): pl.pallas_call(functools.partial(gather_kernel, sizes), out_shape=(jax.Sh...]
    all_to_all x1 -> x0, waiting for transfers between devices: 72.2 us -> none  [return_rows(): lax.all_to_all(fetched, ('index', 'bulk'), split_axis=0, concat_axis=0, t...]
    psum x1 -> x0, blocking collectives: 37.1 us -> none  [body(): summed = lax.psum(jnp.sum(divergence), ('index', 'bulk'))]
    gather x2 -> x0, local copies, waits for them, and re-layouts: 17.2 us -> none  [the longest x1 9.38 us: body(): fetched = jnp.take(passages, wanted, axis=0)]
    all_to_all x1 -> x0, blocking collectives: 14.2 us -> none  [send_requests(): lax.all_to_all(request, ('index', 'bulk'), split_axis=0, concat_axis=0, t...]
    another operation x3 -> x0, other arithmetic: 9.15 us -> none
    scatter x1 -> x0, local copies, waits for them, and re-layouts: 4.32 us -> none  [body(): jnp.zeros((owners * capacity,), jnp.int32).at[send_slot].set(row_of)]
    all_to_all x1 -> x0, starting transfers between devices: 3.65 us -> none  [return_rows(): lax.all_to_all(fetched, ('index', 'bulk'), split_axis=0, concat_axis=0, t...]
  transfers between devices with their start and end apart: 1 -> 0, of which waited for: 1 -> 0; matrix products, arithmetic and copies ran while one was open for 0% -> 0% of each run, Pallas kernels for 0% -> 0%
where the time goes in v1:
time: 98.8 us; the launch traced here: 98.4 us
  Pallas kernels  91.6 us (93%)
  local copies, waits for them, and re-layouts  4.3 us (4%)
  between operations  2.47 us (3%)
    pallas_call x1, Pallas kernels, body(): pl.pallas_call(functools.partial(gather_kernel, sizes), out_shape=(jax.Sh...  22.7 us
    pallas_call x1, Pallas kernels, body(): pl.pallas_call(functools.partial(reduce_kernel, sizes, scale), out_shape=...  21.8 us
    pallas_call x1, Pallas kernels, body(): pl.pallas_call(functools.partial(weight_kernel, sizes, k, scale), out_sha...  20.1 us
    pallas_call x1, Pallas kernels, body(): pl.pallas_call(functools.partial(grad_kernel, sizes, chunk, k), out_shape...  15.4 us
    pallas_call x1, Pallas kernels, body(): pl.pallas_call(functools.partial(score_kernel, sizes, chunk, k), out_shap...  11.6 us

profile of v1, /device:TPU:0, one launch (start us, length us, event | category | flops | bytes accessed | tf_op | source)
XLA Modules:
  0.0 98.4 jit_solution(12161068458398629469)
XLA Ops:
  0.6 1.4 %reshape.10.id_ref = s32[8,128]{1,0:T(8,128)} reshape(s32[32,32]{1,0:T(8,128)} %param.6) | data formatting | bytes 8192 | tf_op jit(solution)/shard_map/reshape | solution.py:334
  2.0 1.4 %reshape.11.reader = f32[8,128]{1,0:T(8,128)} reshape(f32[32,32]{1,0:T(8,128)} %param.7) | data formatting | bytes 8192 | tf_op jit(solution)/shard_map/reshape | solution.py:335
  3.4 22.7 %gather_questions.1 = (bf16[1024,768]{1,0:T(8,128)(2,1)}, s32[256,128]{1,0:T(8,128)}) custom-call(bf16[32,768]{1,0:T(8,128)(2,1)} %q_ref.1, s32[8,128]{1,0:T(8,128)} %reshape.10.id_ref), custom_call_target="tpu_custom_call" | custom-call | tf_op jit(solution)/shard_map/gather_questions/pallas_call | solution.py:339
  26.1 11.6 %owner_scores.1.ps = f32[256,128]{1,0:T(8,128)} custom-call(bf16[1024,768]{1,0:T(8,128)(2,1)} %get-tuple-element.6.qall, bf16[2048,768]{1,0:T(8,128)(2,1)} %p_ref.3, s32[256,128]{1,0:T(8,128)} %get-tuple-element.7.idall), custom_call_target="tpu_custom_call" | custom-call | tf_op jit(solution)/shard_map/owner_scores/pallas_call | solution.py:347
  37.7 20.1 %exchange_weights.1 = (f32[256,128]{1,0:T(8,128)}, f32[1,1]{1,0:T(1,128)}) custom-call(f32[256,128]{1,0:T(8,128)} %owner_scores.1.ps, f32[8,128]{1,0:T(8,128)} %reshape.11.reader), custom_call_target="tpu_custom_call" | custom-call | tf_op jit(solution)/shard_map/exchange_weights/pallas_call | solution.py:354
  57.8 15.4 %owner_grads.1.g_ref = f32[1024,768]{1,0:T(8,128)} custom-call(f32[256,128]{1,0:T(8,128)} %get-tuple-element.9.wall, bf16[2048,768]{1,0:T(8,128)(2,1)} %p_ref.3, s32[256,128]{1,0:T(8,128)} %get-tuple-element.7.idall), custom_call_target="tpu_custom_call" | custom-call | tf_op jit(solution)/shard_map/owner_grads/pallas_call | solution.py:365
  73.2 21.8 %reduce_grads.1 = f32[32,768]{1,0:T(8,128)} custom-call(f32[1024,768]{1,0:T(8,128)} %owner_grads.1.g_ref), custom_call_target="tpu_custom_call" | custom-call | tf_op jit(solution)/shard_map/reduce_grads/pallas_call | solution.py:373
  95.7 1.5 %copy.9 = f32[32,768]{1,0:T(8,128)} copy(f32[32,768]{1,0:T(8,128)} %reduce_grads.1) | data formatting | bytes 196608

commit v2 on v0

v2 whole, which is shorter than its diff:
```python
import functools
import math

import jax
import jax.numpy as jnp
from jax import lax
from jax.experimental import pallas as pl
from jax.experimental.pallas import tpu as pltpu
from jax.sharding import PartitionSpec as P

MESH = pl.DeviceIdType.MESH
LANES = 128
SUB = 8
VMEM_LIMIT = 60 * 1024 * 1024


class Place:
    def __init__(self, sizes):
        self.ny, self.nz, self.nx = sizes
        self.flat = self.ny * self.nx
        self.chunk = 2 * self.flat
        self.n = self.chunk * self.nz
        index, bulk = lax.axis_index("index"), lax.axis_index("bulk")
        self.y, self.c = index // 2, index % 2
        self.z, self.x = bulk // self.nx, bulk % self.nx
        self.me = self.position(self.z, self.c, self.y, self.x)
        self.owner = index * self.nz * self.nx + bulk

    def position(self, z, c, y, x):
        return (z * 2 + c) * self.flat + y * self.nx + x

    def device(self, z, c, y, x):
        return (y * 2 + c, z * self.nx + x)

    def device_at(self, position):
        z, rest = position // self.chunk, position % self.chunk
        c, rest = rest // self.flat, rest % self.flat
        return self.device(z, c, rest // self.nx, rest % self.nx)

    def plane(self):
        for a in range(self.ny):
            for b in range(self.nx):
                if a or b:
                    yield (a * self.nx + b, (self.y + a) % self.ny, (self.x + b) % self.nx)


def wait_bytes(ref, sem):
    pltpu.make_async_copy(ref, ref, sem).wait()


def grouped(x, k, reduce, empty):
    group = lax.broadcasted_iota(jnp.int32, x.shape, 1) // k
    result = jnp.full(x.shape, empty, x.dtype)
    for j in range(x.shape[1] // k):
        value = reduce(jnp.where(group == j, x, empty), axis=1, keepdims=True)
        result = jnp.where(group == j, value, result)
    return result


def log_normalize(x, k):
    shifted = x - grouped(x, k, jnp.max, -jnp.inf)
    return shifted - jnp.log(grouped(jnp.exp(shifted), k, jnp.sum, 0.0))


def kernel(sizes, scale, hold, q_ref, p_hbm, id_ref, reader_ref, out, mean,
           p_ref, qall, idall, s, ps, srecv, mine, mall, onehot, wd, g, sib, acc, going, coming, zin, perm,
           p_sem, q_send, q_recv, id_send, id_recv, s_send, s_recv, w_send, w_recv,
           sib_send, sib_recv, p_send, p_recv, z_send, z_recv):
    t = Place(sizes)
    rows, k = id_ref.shape
    per, width = p_ref.shape
    tiles, group = per // LANES, LANES // k
    r8 = rows // group
    pair = 8 // group
    half = t.flat * rows
    f32, bf16 = jnp.float32, jnp.bfloat16

    def span(number, count):
        return pl.ds(pl.multiple_of(number * count, count), count)

    load = pltpu.make_async_copy(p_hbm, p_ref, p_sem)
    load.start()
    barrier = pltpu.get_barrier_semaphore()

    def greet(i, carry):
        pl.semaphore_signal(
            barrier, inc=1, device_id=t.device_at((t.me + i) % t.n), device_id_type=MESH)
        return carry

    lax.fori_loop(1, t.n, greet, 0)

    def packed(ref):
        return jnp.concatenate([ref[j * r8:(j + 1) * r8, :] for j in range(group)], axis=1)

    idall[span(t.me, r8), :] = packed(id_ref)
    qall[span(t.me, rows), :] = q_ref[...]
    log_reader = log_normalize(packed(reader_ref), k)
    reader_prob = jnp.exp(log_reader)
    pl.semaphore_wait(barrier, t.n - 1)

    def to_all(src, dst, send_sem, recv_sem):
        def send(i, carry):
            pltpu.make_async_remote_copy(
                src_ref=src, dst_ref=dst, send_sem=send_sem, recv_sem=recv_sem,
                device_id=t.device_at((t.me + i) % t.n), device_id_type=MESH,
            ).start()
            return carry

        lax.fori_loop(1, t.n, send, 0)

    def block(position):
        return qall.at[span(position, rows)]

    def give(src, position, device):
        pltpu.make_async_remote_copy(
            src_ref=src, dst_ref=block(position), send_sem=q_send, recv_sem=q_recv.at[position],
            device_id=device, device_id_type=MESH,
        ).start()

    def arrived(position):
        wait_bytes(block(position), q_recv.at[position])

    sibling = t.device(t.z, 1 - t.c, t.y, t.x)
    for i in range(1, t.nz):
        give(q_ref, t.me, t.device((t.z + i) % t.nz, t.c, t.y, t.x))
    for _, y, x in t.plane():
        give(q_ref, t.me, t.device(t.z, t.c, y, x))
    give(q_ref, t.me, sibling)
    to_all(idall.at[span(t.me, r8)], idall.at[span(t.me, r8)], id_send, id_recv)

    def pass_plane(i):
        for _, y, x in t.plane():
            position = t.position((t.z + i) % t.nz, t.c, y, x)
            arrived(position)
            give(block(position), position, sibling)

    pass_plane(0)
    for i in range(1, t.nz):
        position = t.position((t.z + i) % t.nz, t.c, t.y, t.x)
        arrived(position)
        for _, y, x in t.plane():
            give(block(position), position, t.device(t.z, t.c, y, x))
        give(block(position), position, sibling)
    wait_bytes(idall.at[pl.ds(0, (t.n - 1) * r8)], id_recv)
    load.wait()

    lane_group = lax.broadcasted_iota(jnp.int32, (r8, LANES), 1) // k
    row_part = lax.broadcasted_iota(jnp.int32, (r8, LANES), 0) % pair

    def parts_of(position):
        local = idall[span(position, r8), :] - t.owner * per
        own = (local >= 0) & (local < per)
        return own, local // LANES, local & (LANES - 1)

    def score(base):
        def one_sub(u, carry):
            first = base + u * SUB
            q = qall[pl.ds(pl.multiple_of(first * rows, SUB * rows), SUB * rows), :]
            for h in range(0, tiles, 2):
                both = lax.dot_general(
                    q, p_ref[h * LANES:(h + 2) * LANES, :],
                    (((1,), (1,)), ((), ())), preferred_element_type=f32)
                s[h] = both[:, :LANES]
                s[h + 1] = both[:, LANES:]

            def one_device(i, carry):
                position = first + i
                own, high, low = parts_of(position)
                code = jnp.where(own, lane_group * tiles + high, -1)
                total = jnp.zeros((r8, LANES), f32)
                for j in range(group):
                    for h in range(tiles):
                        piece = s[h, pl.ds(pl.multiple_of(i * rows + j * r8, r8), r8), :]
                        picked = jnp.take_along_axis(piece, low, axis=1)
                        total = jnp.where(code == j * tiles + h, picked, total)
                ps[span(position, r8), :] = total

                @pl.when(position != t.me)
                def _():
                    pltpu.make_async_remote_copy(
                        src_ref=ps.at[span(position, r8)], dst_ref=srecv.at[span(t.me, r8)],
                        send_sem=s_send, recv_sem=s_recv,
                        device_id=t.device_at(position), device_id_type=MESH,
                    ).start()

                @pl.when(position == t.me)
                def _():
                    srecv[span(t.me, r8), :] = total

                return carry

            return lax.fori_loop(0, SUB, one_device, carry)

        lax.fori_loop(0, t.chunk // SUB, one_sub, 0)

    for i in range(t.nz):
        if i + 1 < t.nz:
            pass_plane(i + 1)
        z = (t.z + i) % t.nz
        arrived(t.position(z, 1 - t.c, t.y, t.x))
        for _, y, x in t.plane():
            arrived(t.position(z, 1 - t.c, y, x))
        score(z * t.chunk)

    iota16 = lax.broadcasted_iota(jnp.int32, (16, LANES), 0)

    def spread(row):
        return jnp.broadcast_to(row, (16, LANES)).astype(bf16)

    one, zero = jnp.ones((16, LANES), bf16), jnp.zeros((16, LANES), bf16)

    def column(m):
        return (iota16 + 16 * m).astype(f32).astype(bf16)

    def build(base, slot):
        def one_device(i, carry):
            _, _, low = parts_of(base + i)
            low = low.astype(f32)
            for b in range(r8):
                row = spread(low[b:b + 1, :])
                at = pl.ds(pl.multiple_of(((slot + i) * (r8 // pair) + b // pair) * LANES, LANES), LANES)
                onehot[at, (b % pair) * LANES:(b % pair + 1) * LANES] = jnp.concatenate(
                    [jnp.where(column(m) == row, one, zero) for m in range(LANES // 16)],
                    axis=0)
            return carry

        lax.fori_loop(0, t.chunk, one_device, 0)

    order = list(range(1, t.nz)) + [0]

    def early(indices):
        if hold:
            for i in indices:
                z = (t.z + i) % t.nz
                build(z * t.chunk, z * t.chunk)

    early(order[:t.nz // 2])

    wait_bytes(srecv.at[pl.ds(0, (t.n - 1) * r8)], s_recv)
    scores = jnp.sum(srecv[...].reshape(t.n, r8, LANES), axis=0) * scale
    log_retriever = log_normalize(scores, k)
    weights = (jnp.exp(log_retriever) - reader_prob).astype(bf16).astype(f32)
    mine[0:r8, :] = weights
    mine[r8:2 * r8, :] = reader_prob * (log_reader - log_retriever)
    to_all(mine, mall.at[span(t.me, 2 * r8)], w_send, w_recv)
    mall[span(t.me, 2 * r8), :] = mine[...]
    early(order[t.nz // 2:])
    wait_bytes(mall.at[pl.ds(0, (t.n - 1) * 2 * r8)], w_recv)

    def grads(i):
        base = (t.z + i) % t.nz * t.chunk
        if not hold:
            build(base, 0)

        def one_sub(u, carry):
            def one_device(v, carry):
                position = base + u * SUB + v
                slot = position if hold else u * SUB + v
                own, high, _ = parts_of(position)
                code = jnp.where(own, high * 8 + row_part * group + lane_group, -1).astype(f32)
                w = mall[pl.ds(pl.multiple_of(position * 2 * r8, 2 * r8), r8), :]
                for a in range(0, r8 // pair, 2):
                    dense = []
                    for e in (a, a + 1):
                        left = []
                        for b in range(e * pair, (e + 1) * pair):
                            codes, values = spread(code[b:b + 1, :]), spread(w[b:b + 1, :])
                            left.append(jnp.concatenate(
                                [jnp.where(column(m) == codes, values, zero)
                                 for m in range(8 * tiles // 16)], axis=0))
                        right = onehot[pl.ds(pl.multiple_of((slot * (r8 // pair) + e) * LANES, LANES), LANES), :]
                        dense.append(lax.dot_general(
                            jnp.concatenate(left, axis=1), right,
                            (((1,), (1,)), ((), ())), preferred_element_type=f32))
                    to = pl.ds(pl.multiple_of(v * rows + a * 8, 16), 16)
                    for h in range(tiles):
                        wd[to, h * LANES:(h + 1) * LANES] = jnp.concatenate(
                            [d[h * 8:(h + 1) * 8, :] for d in dense], axis=0).astype(bf16)
                return carry

            lax.fori_loop(0, SUB, one_device, 0)
            g[i, pl.ds(pl.multiple_of(u * SUB * rows, SUB * rows), SUB * rows), :] = jnp.dot(
                wd[...], p_ref[...], preferred_element_type=f32)
            return carry

        lax.fori_loop(0, t.chunk // SUB, one_sub, 0)
        copy = pltpu.make_async_remote_copy(
            src_ref=g.at[i, span(1 - t.c, half)], dst_ref=sib.at[i],
            send_sem=sib_send.at[i], recv_sem=sib_recv.at[i],
            device_id=sibling, device_id_type=MESH)
        copy.start()
        return copy

    firsts, seconds, thirds = {}, {}, {}

    def summed(i, y, x):
        number = y * t.nx + x
        return (g[i, pl.ds(pl.multiple_of(t.c * half + number * rows, rows), rows), :]
                + sib[i, span(number, rows), :])

    def in_plane(i):
        firsts[i].wait_recv()
        for o, y, x in t.plane():
            going[i, o] = summed(i, y, x).astype(bf16)
            copy = pltpu.make_async_remote_copy(
                src_ref=going.at[i, o], dst_ref=coming.at[i, o],
                send_sem=p_send.at[i, o], recv_sem=p_recv.at[i, o],
                device_id=t.device(t.z, t.c, y, x), device_id_type=MESH)
            copy.start()
            seconds[i, o] = copy
        acc[i] = summed(i, t.y, t.x)

    def along_z(i):
        total = acc[i]
        for o, _, _ in t.plane():
            seconds[i, o].wait_recv()
            total = total + coming[i, o].astype(f32)
        acc[i] = total
        if i:
            copy = pltpu.make_async_remote_copy(
                src_ref=acc.at[i], dst_ref=zin.at[i],
                send_sem=z_send.at[i], recv_sem=z_recv.at[i],
                device_id=t.device((t.z + i) % t.nz, t.c, t.y, t.x), device_id_type=MESH)
            copy.start()
            thirds[i] = copy

    for step in range(t.nz + 2):
        if step < t.nz:
            firsts[order[step]] = grads(order[step])
        if 1 <= step <= t.nz:
            in_plane(order[step - 1])
        if 2 <= step:
            along_z(order[step - 2])
    total = acc[0]
    for i, copy in thirds.items():
        copy.wait_recv()
        total = total + zin[i]
    for l in range(width // LANES):
        perm[l] = total[:, l * LANES:(l + 1) * LANES]
    for l in range(width // LANES):
        for j in range(group):
            out[j * r8:(j + 1) * r8, l * LANES:(l + 1) * LANES] = perm[l, pl.ds(j, r8, stride=group), :]
    divergence = mall[...].reshape(t.n, 2 * r8, LANES)[:, r8:, :]
    mean[0, 0] = jnp.sum(jnp.sum(divergence, axis=0)) / (t.n * rows)

    wait_bytes(qall.at[pl.ds(0, (t.n - 1) * rows)], q_send)
    wait_bytes(idall.at[pl.ds(0, (t.n - 1) * r8)], id_send)
    wait_bytes(srecv.at[pl.ds(0, (t.n - 1) * r8)], s_send)
    wait_bytes(mall.at[pl.ds(0, (t.n - 1) * 2 * r8)], w_send)
    for copies in (firsts, seconds, thirds):
        for copy in copies.values():
            copy.wait_send()


def solution(mesh):
    n_index, n_bulk = mesh.shape["index"], mesh.shape["bulk"]
    ny = n_index // 2
    nx = math.gcd(ny, n_bulk)
    nz = n_bulk // nx
    flat = ny * nx
    n = n_index * n_bulk
    vmem = pl.BlockSpec(memory_space=pltpu.VMEM)
    dma = pltpu.SemaphoreType.DMA

    def body(questions, passages, candidate_ids, reader_loglik):
        rows, k = candidate_ids.shape
        per, width = passages.shape
        r8 = rows * k // LANES
        scale = 4.0 / math.sqrt(width)
        f32, bf16, i32 = jnp.float32, jnp.bfloat16, jnp.int32
        hold = n * rows * k * LANES * 2 <= 12 * 1024 * 1024
        held = n if hold else 2 * flat
        grads, mean = pl.pallas_call(
            functools.partial(kernel, (ny, nz, nx), scale, hold),
            out_shape=(jax.ShapeDtypeStruct((rows, width), f32), jax.ShapeDtypeStruct((1, 1), f32)),
            in_specs=[vmem, pl.BlockSpec(memory_space=pl.ANY), vmem, vmem],
            out_specs=(vmem, pl.BlockSpec(memory_space=pltpu.SMEM)),
            scratch_shapes=[
                pltpu.VMEM((per, width), bf16),
                pltpu.VMEM((n * rows, width), bf16),
                pltpu.VMEM((n * r8, LANES), i32),
                pltpu.VMEM((per // LANES, SUB * rows, LANES), f32),
                pltpu.VMEM((n * r8, LANES), f32),
                pltpu.VMEM((n * r8, LANES), f32),
                pltpu.VMEM((2 * r8, LANES), f32),
                pltpu.VMEM((n * 2 * r8, LANES), f32),
                pltpu.VMEM((held * rows * k // 2, 2 * LANES), bf16),
                pltpu.VMEM((SUB * rows, per), bf16),
                pltpu.VMEM((nz, 2 * flat * rows, width), f32),
                pltpu.VMEM((nz, flat * rows, width), f32),
                pltpu.VMEM((nz, rows, width), f32),
                pltpu.VMEM((nz, flat, rows, width), bf16),
                pltpu.VMEM((nz, flat, rows, width), bf16),
                pltpu.VMEM((nz, rows, width), f32),
                pltpu.VMEM((width // LANES, rows, LANES), f32),
                dma, dma, dma((n,)), dma, dma, dma, dma, dma, dma,
                dma((nz,)), dma((nz,)), dma((nz, flat)), dma((nz, flat)), dma((nz,)), dma((nz,)),
            ],
            compiler_params=pltpu.CompilerParams(
                collective_id=0, has_side_effects=True, vmem_limit_bytes=VMEM_LIMIT),
            name="retriever_step",
        )(questions, passages, candidate_ids, reader_loglik)
        return mean[0, 0], grads * scale

    placed = P(("index", "bulk"), None)
    return jax.shard_map(
        body, mesh=mesh, in_specs=(placed,) * 4, out_specs=(P(), placed), check_vma=False)
```

time: 174 us -> 66.4 us (0.38)
  waiting for transfers between devices: 72.2 us -> 0 us
  Pallas kernels: 0 us -> 62.1 us
  blocking collectives: 51.3 us -> 0 us
  local copies, waits for them, and re-layouts: 25.2 us -> 0 us
  other arithmetic: 15.3 us -> 1.54 us
  starting transfers between devices: 3.65 us -> 0 us
  matrix products: 2.5 us -> 0 us
    all_to_all x1 -> x0, waiting for transfers between devices: 72.2 us -> none  [return_rows(): lax.all_to_all(fetched, ('index', 'bulk'), split_axis=0, concat_axis=0, t...]
    pallas_call x0 -> x1, Pallas kernels: none -> 62.1 us  [body(): pl.pallas_call(functools.partial(kernel, (ny, nz, nx), scale, hold), out_...]
    psum x1 -> x0, blocking collectives: 37.1 us -> none  [body(): summed = lax.psum(jnp.sum(divergence), ('index', 'bulk'))]
    gather x2 -> x0, local copies, waits for them, and re-layouts: 17.2 us -> none  [the longest x1 9.38 us: body(): fetched = jnp.take(passages, wanted, axis=0)]
    all_to_all x1 -> x0, blocking collectives: 14.2 us -> none  [send_requests(): lax.all_to_all(request, ('index', 'bulk'), split_axis=0, concat_axis=0, t...]
    another operation x3 -> x0, other arithmetic: 9.15 us -> none
    scatter x1 -> x0, local copies, waits for them, and re-layouts: 4.32 us -> none  [body(): jnp.zeros((owners * capacity,), jnp.int32).at[send_slot].set(row_of)]
    all_to_all x1 -> x0, starting transfers between devices: 3.65 us -> none  [return_rows(): lax.all_to_all(fetched, ('index', 'bulk'), split_axis=0, concat_axis=0, t...]
  transfers between devices with their start and end apart: 1 -> 0, of which waited for: 1 -> 0; matrix products, arithmetic and copies ran while one was open for 0% -> 0% of each run, Pallas kernels for 0% -> 0%
where the time goes in v2:
time: 66.4 us; the launch traced here: 66.1 us
  Pallas kernels  62.1 us (94%)
  between operations  2.46 us (4%)
  other arithmetic  1.54 us (2%)
    pallas_call x1, Pallas kernels, body(): pl.pallas_call(functools.partial(kernel, (ny, nz, nx), scale, hold), out_...  62.1 us
    mul x1, other arithmetic, body(): return (mean[0, 0], grads * scale)  1.54 us

profile of v2, /device:TPU:0, one launch (start us, length us, event | category | flops | bytes accessed | tf_op | source)
XLA Modules:
  0.0 66.1 jit_solution(5150036619638443766)
XLA Ops:
  0.6 62.1 %retriever_step.1 = (f32[32,768]{1,0:T(8,128)}, f32[1,1]{1,0:T(1,128)}) custom-call(bf16[32,768]{1,0:T(8,128)(2,1)} %q_ref.1, bf16[2048,768]{1,0:T(8,128)(2,1)} %p_hbm.1, s32[32,32]{1,0:T(8,128)} %id_ref.1, f32[32,32]{1,0:T(8,128)} %reader_ref.1), custom_call_target="tpu_custom_call" | custom-call | tf_op jit(solution)/shard_map/retriever_step/pallas_call | solution.py:373
  62.7 1.5 %broadcast_multiply_fusion = f32[32,768]{1,0:T(8,128)} fusion(f32[32,768]{1,0:T(8,128)} %get-tuple-element.5), kind=kLoop, calls=%fused_computation | loop fusion | flops 24576 | bytes 196608 | tf_op jit(solution)/shard_map/mul | solution.py:403

commit v3 on v2

--- a/solution.py
+++ b/solution.py
@@ -11,7 +11,7 @@
 MESH = pl.DeviceIdType.MESH
 LANES = 128
 SUB = 8
-VMEM_LIMIT = 60 * 1024 * 1024
+VMEM_LIMIT = 58 * 1024 * 1024
 
 
 class Place:
@@ -32,10 +32,22 @@
     def device(self, z, c, y, x):
         return (y * 2 + c, z * self.nx + x)
 
-    def device_at(self, position):
-        z, rest = position // self.chunk, position % self.chunk
-        c, rest = rest // self.flat, rest % self.flat
-        return self.device(z, c, rest // self.nx, rest % self.nx)
+    def others(self, act):
+        def one_plane(i, carry):
+            z = lax.rem(self.z + i, self.nz)
+            for c in (self.c, 1 - self.c):
+                for a in range(self.ny):
+                    for b in range(self.nx):
+                        y, x = lax.rem(self.y + a, self.ny), lax.rem(self.x + b, self.nx)
+                        if c is self.c and a == 0 and b == 0:
+                            @pl.when(i > 0)
+                            def _():
+                                act(self.device(z, c, y, x))
+                        else:
+                            act(self.device(z, c, y, x))
+            return carry
+
+        lax.fori_loop(0, self.nz, one_plane, 0)
 
     def plane(self):
         for a in range(self.ny):
@@ -62,9 +74,9 @@
     return shifted - jnp.log(grouped(jnp.exp(shifted), k, jnp.sum, 0.0))
 
 
-def kernel(sizes, scale, hold, q_ref, p_hbm, id_ref, reader_ref, out, mean,
-           p_ref, qall, idall, s, ps, srecv, mine, mall, onehot, wd, g, sib, acc, going, coming, zin, perm,
-           p_sem, q_send, q_recv, id_send, id_recv, s_send, s_recv, w_send, w_recv,
+def kernel(sizes, scale, hold, q_hbm, p_hbm, id_hbm, reader_hbm, out, mean,
+           p_ref, id_ref, reader_ref, qall, idall, s, ps, srecv, mine, mall, onehot, wd, g, sib, acc, going, coming, zin, perm,
+           p_sem, in_sem, q_send, q_recv, id_send, id_recv, s_send, s_recv, w_send, w_recv,
            sib_send, sib_recv, p_send, p_recv, z_send, z_recv):
     t = Place(sizes)
     rows, k = id_ref.shape
@@ -78,35 +90,34 @@
     def span(number, count):
         return pl.ds(pl.multiple_of(number * count, count), count)
 
+    mine_in = [
+        pltpu.make_async_copy(id_hbm, id_ref, in_sem.at[0]),
+        pltpu.make_async_copy(reader_hbm, reader_ref, in_sem.at[1]),
+        pltpu.make_async_copy(q_hbm, qall.at[span(t.me, rows)], in_sem.at[2]),
+    ]
+    for copy in mine_in:
+        copy.start()
     load = pltpu.make_async_copy(p_hbm, p_ref, p_sem)
     load.start()
     barrier = pltpu.get_barrier_semaphore()
 
-    def greet(i, carry):
-        pl.semaphore_signal(
-            barrier, inc=1, device_id=t.device_at((t.me + i) % t.n), device_id_type=MESH)
-        return carry
-
-    lax.fori_loop(1, t.n, greet, 0)
+    t.others(lambda device: pl.semaphore_signal(
+        barrier, inc=1, device_id=device, device_id_type=MESH))
 
     def packed(ref):
         return jnp.concatenate([ref[j * r8:(j + 1) * r8, :] for j in range(group)], axis=1)
 
+    for copy in mine_in:
+        copy.wait()
     idall[span(t.me, r8), :] = packed(id_ref)
-    qall[span(t.me, rows), :] = q_ref[...]
     log_reader = log_normalize(packed(reader_ref), k)
     reader_prob = jnp.exp(log_reader)
     pl.semaphore_wait(barrier, t.n - 1)
 
     def to_all(src, dst, send_sem, recv_sem):
-        def send(i, carry):
-            pltpu.make_async_remote_copy(
-                src_ref=src, dst_ref=dst, send_sem=send_sem, recv_sem=recv_sem,
-                device_id=t.device_at((t.me + i) % t.n), device_id_type=MESH,
-            ).start()
-            return carry
-
-        lax.fori_loop(1, t.n, send, 0)
+        t.others(lambda device: pltpu.make_async_remote_copy(
+            src_ref=src, dst_ref=dst, send_sem=send_sem, recv_sem=recv_sem,
+            device_id=device, device_id_type=MESH).start())
 
     def block(position):
         return qall.at[span(position, rows)]
@@ -122,10 +133,10 @@
 
     sibling = t.device(t.z, 1 - t.c, t.y, t.x)
     for i in range(1, t.nz):
-        give(q_ref, t.me, t.device((t.z + i) % t.nz, t.c, t.y, t.x))
+        give(block(t.me), t.me, t.device((t.z + i) % t.nz, t.c, t.y, t.x))
     for _, y, x in t.plane():
-        give(q_ref, t.me, t.device(t.z, t.c, y, x))
-    give(q_ref, t.me, sibling)
+        give(block(t.me), t.me, t.device(t.z, t.c, y, x))
+    give(block(t.me), t.me, sibling)
     to_all(idall.at[span(t.me, r8)], idall.at[span(t.me, r8)], id_send, id_recv)
 
     def pass_plane(i):
@@ -152,55 +163,59 @@
         own = (local >= 0) & (local < per)
         return own, local // LANES, local & (LANES - 1)
 
-    def score(base):
+    def score(z):
         def one_sub(u, carry):
-            first = base + u * SUB
+            first = z * t.chunk + u * SUB
             q = qall[pl.ds(pl.multiple_of(first * rows, SUB * rows), SUB * rows), :]
+            codes, lows, totals = [], [], [None] * SUB
+            for i in range(SUB):
+                own, high, low = parts_of(first + i)
+                codes.append(jnp.where(own, lane_group * tiles + high, -1))
+                lows.append(low)
             for h in range(0, tiles, 2):
-                both = lax.dot_general(
+                s[h // 2] = lax.dot_general(
                     q, p_ref[h * LANES:(h + 2) * LANES, :],
                     (((1,), (1,)), ((), ())), preferred_element_type=f32)
-                s[h] = both[:, :LANES]
-                s[h + 1] = both[:, LANES:]
-
-            def one_device(i, carry):
-                position = first + i
-                own, high, low = parts_of(position)
-                code = jnp.where(own, lane_group * tiles + high, -1)
-                total = jnp.zeros((r8, LANES), f32)
-                for j in range(group):
-                    for h in range(tiles):
-                        piece = s[h, pl.ds(pl.multiple_of(i * rows + j * r8, r8), r8), :]
-                        picked = jnp.take_along_axis(piece, low, axis=1)
-                        total = jnp.where(code == j * tiles + h, picked, total)
-                ps[span(position, r8), :] = total
-
-                @pl.when(position != t.me)
-                def _():
-                    pltpu.make_async_remote_copy(
-                        src_ref=ps.at[span(position, r8)], dst_ref=srecv.at[span(t.me, r8)],
-                        send_sem=s_send, recv_sem=s_recv,
-                        device_id=t.device_at(position), device_id_type=MESH,
-                    ).start()
-
-                @pl.when(position == t.me)
-                def _():
-                    srecv[span(t.me, r8), :] = total
-
-                return carry
-
-            return lax.fori_loop(0, SUB, one_device, carry)
+            for h in range(tiles):
+                for i in range(SUB):
+                    for j in range(group):
+                        piece = s[h // 2, i * rows + j * r8:i * rows + (j + 1) * r8,
+                                  h % 2 * LANES:(h % 2 + 1) * LANES]
+                        picked = jnp.take_along_axis(piece, lows[i], axis=1)
+                        picked = jnp.where(codes[i] == j * tiles + h, picked, 0.0)
+                        totals[i] = picked if totals[i] is None else totals[i] + picked
+            for i in range(SUB):
+                ps[span(first + i, r8), :] = totals[i]
+            return carry
 
         lax.fori_loop(0, t.chunk // SUB, one_sub, 0)
-
-    for i in range(t.nz):
-        if i + 1 < t.nz:
+        for c in range(2):
+            for y in range(t.ny):
+                for x in range(t.nx):
+                    position = t.position(z, c, y, x)
+
+                    @pl.when(position != t.me)
+                    def _():
+                        pltpu.make_async_remote_copy(
+                            src_ref=ps.at[span(position, r8)], dst_ref=srecv.at[span(t.me, r8)],
+                            send_sem=s_send, recv_sem=s_recv,
+                            device_id=t.device(z, c, y, x), device_id_type=MESH,
+                        ).start()
+
+    def one_plane(i, carry):
+        @pl.when(i + 1 < t.nz)
+        def _():
             pass_plane(i + 1)
-        z = (t.z + i) % t.nz
+
+        z = lax.rem(t.z + i, t.nz)
         arrived(t.position(z, 1 - t.c, t.y, t.x))
         for _, y, x in t.plane():
             arrived(t.position(z, 1 - t.c, y, x))
-        score(z * t.chunk)
+        score(z)
+        return carry
+
+    lax.fori_loop(0, t.nz, one_plane, 0)
+    srecv[span(t.me, r8), :] = ps[span(t.me, r8), :]
 
     iota16 = lax.broadcasted_iota(jnp.int32, (16, LANES), 0)
 
@@ -226,15 +241,16 @@
 
         lax.fori_loop(0, t.chunk, one_device, 0)
 
-    order = list(range(1, t.nz)) + [0]
-
-    def early(indices):
+    def early(first, last):
+        def one(i, carry):
+            base = lax.rem(t.z + 1 + i, t.nz) * t.chunk
+            build(base, base)
+            return carry
+
         if hold:
-            for i in indices:
-                z = (t.z + i) % t.nz
-                build(z * t.chunk, z * t.chunk)
-
-    early(order[:t.nz // 2])
+            lax.fori_loop(first, last, one, 0)
+
+    early(0, t.nz // 2)
 
     wait_bytes(srecv.at[pl.ds(0, (t.n - 1) * r8)], s_recv)
     scores = jnp.sum(srecv[...].reshape(t.n, r8, LANES), axis=0) * scale
@@ -244,7 +260,7 @@
     mine[r8:2 * r8, :] = reader_prob * (log_reader - log_retriever)
     to_all(mine, mall.at[span(t.me, 2 * r8)], w_send, w_recv)
     mall[span(t.me, 2 * r8), :] = mine[...]
-    early(order[t.nz // 2:])
+    early(t.nz // 2, t.nz)
     wait_bytes(mall.at[pl.ds(0, (t.n - 1) * 2 * r8)], w_recv)
 
     def grads(i):
@@ -284,14 +300,25 @@
             return carry
 
         lax.fori_loop(0, t.chunk // SUB, one_sub, 0)
-        copy = pltpu.make_async_remote_copy(
+        first(i).start()
+
+    def first(i):
+        return pltpu.make_async_remote_copy(
             src_ref=g.at[i, span(1 - t.c, half)], dst_ref=sib.at[i],
             send_sem=sib_send.at[i], recv_sem=sib_recv.at[i],
             device_id=sibling, device_id_type=MESH)
-        copy.start()
-        return copy
-
-    firsts, seconds, thirds = {}, {}, {}
+
+    def second(i, o, y, x):
+        return pltpu.make_async_remote_copy(
+            src_ref=going.at[i, o], dst_ref=coming.at[i, o],
+            send_sem=p_send.at[i, o], recv_sem=p_recv.at[i, o],
+            device_id=t.device(t.z, t.c, y, x), device_id_type=MESH)
+
+    def third(i):
+        return pltpu.make_async_remote_copy(
+            src_ref=acc.at[i], dst_ref=zin.at[i],
+            send_sem=z_send.at[i], recv_sem=z_recv.at[i],
+            device_id=t.device(lax.rem(t.z + i, t.nz), t.c, t.y, t.x), device_id_type=MESH)
 
     def summed(i, y, x):
         number = y * t.nx + x
@@ -299,57 +326,59 @@
                 + sib[i, span(number, rows), :])
 
     def in_plane(i):
-        firsts[i].wait_recv()
+        first(i).wait_recv()
         for o, y, x in t.plane():
             going[i, o] = summed(i, y, x).astype(bf16)
-            copy = pltpu.make_async_remote_copy(
-                src_ref=going.at[i, o], dst_ref=coming.at[i, o],
-                send_sem=p_send.at[i, o], recv_sem=p_recv.at[i, o],
-                device_id=t.device(t.z, t.c, y, x), device_id_type=MESH)
-            copy.start()
-            seconds[i, o] = copy
+            second(i, o, y, x).start()
         acc[i] = summed(i, t.y, t.x)
 
     def along_z(i):
         total = acc[i]
-        for o, _, _ in t.plane():
-            seconds[i, o].wait_recv()
+        for o, y, x in t.plane():
+            second(i, o, y, x).wait_recv()
             total = total + coming[i, o].astype(f32)
         acc[i] = total
-        if i:
-            copy = pltpu.make_async_remote_copy(
-                src_ref=acc.at[i], dst_ref=zin.at[i],
-                send_sem=z_send.at[i], recv_sem=z_recv.at[i],
-                device_id=t.device((t.z + i) % t.nz, t.c, t.y, t.x), device_id_type=MESH)
-            copy.start()
-            thirds[i] = copy
-
-    for step in range(t.nz + 2):
-        if step < t.nz:
-            firsts[order[step]] = grads(order[step])
-        if 1 <= step <= t.nz:
-            in_plane(order[step - 1])
-        if 2 <= step:
-            along_z(order[step - 2])
+
+    def one_step(step, carry):
+        grads(lax.rem(step + 1, t.nz))
+
+        @pl.when(step >= 1)
+        def _():
+            in_plane(step)
+
+        @pl.when(step >= 2)
+        def _():
+            along_z(step - 1)
+            third(step - 1).start()
+
+        return carry
+
+    lax.fori_loop(0, t.nz, one_step, 0)
+    in_plane(0)
+    along_z(t.nz - 1)
+    third(t.nz - 1).start()
+    divergence = mall[...].reshape(t.n, 2 * r8, LANES)[:, r8:, :]
+    mean[0, 0] = jnp.sum(jnp.sum(divergence, axis=0)) / (t.n * rows)
+    along_z(0)
     total = acc[0]
-    for i, copy in thirds.items():
-        copy.wait_recv()
+    for i in range(1, t.nz):
+        third(i).wait_recv()
         total = total + zin[i]
     for l in range(width // LANES):
         perm[l] = total[:, l * LANES:(l + 1) * LANES]
     for l in range(width // LANES):
         for j in range(group):
             out[j * r8:(j + 1) * r8, l * LANES:(l + 1) * LANES] = perm[l, pl.ds(j, r8, stride=group), :]
-    divergence = mall[...].reshape(t.n, 2 * r8, LANES)[:, r8:, :]
-    mean[0, 0] = jnp.sum(jnp.sum(divergence, axis=0)) / (t.n * rows)
-
     wait_bytes(qall.at[pl.ds(0, (t.n - 1) * rows)], q_send)
     wait_bytes(idall.at[pl.ds(0, (t.n - 1) * r8)], id_send)
     wait_bytes(srecv.at[pl.ds(0, (t.n - 1) * r8)], s_send)
     wait_bytes(mall.at[pl.ds(0, (t.n - 1) * 2 * r8)], w_send)
-    for copies in (firsts, seconds, thirds):
-        for copy in copies.values():
-            copy.wait_send()
+    for i in range(t.nz):
+        first(i).wait_send()
+        for o, y, x in t.plane():
+            second(i, o, y, x).wait_send()
+        if i:
+            third(i).wait_send()
 
 
 def solution(mesh):
@@ -373,13 +402,15 @@
         grads, mean = pl.pallas_call(
             functools.partial(kernel, (ny, nz, nx), scale, hold),
             out_shape=(jax.ShapeDtypeStruct((rows, width), f32), jax.ShapeDtypeStruct((1, 1), f32)),
-            in_specs=[vmem, pl.BlockSpec(memory_space=pl.ANY), vmem, vmem],
+            in_specs=[pl.BlockSpec(memory_space=pl.ANY)] * 4,
             out_specs=(vmem, pl.BlockSpec(memory_space=pltpu.SMEM)),
             scratch_shapes=[
                 pltpu.VMEM((per, width), bf16),
+                pltpu.VMEM((rows, k), i32),
+                pltpu.VMEM((rows, k), f32),
                 pltpu.VMEM((n * rows, width), bf16),
                 pltpu.VMEM((n * r8, LANES), i32),
-                pltpu.VMEM((per // LANES, SUB * rows, LANES), f32),
+                pltpu.VMEM((per // LANES // 2, SUB * rows, 2 * LANES), f32),
                 pltpu.VMEM((n * r8, LANES), f32),
                 pltpu.VMEM((n * r8, LANES), f32),
                 pltpu.VMEM((2 * r8, LANES), f32),
@@ -393,7 +424,7 @@
                 pltpu.VMEM((nz, flat, rows, width), bf16),
                 pltpu.VMEM((nz, rows, width), f32),
                 pltpu.VMEM((width // LANES, rows, LANES), f32),
-                dma, dma, dma((n,)), dma, dma, dma, dma, dma, dma,
+                dma, dma((3,)), dma, dma((n,)), dma, dma, dma, dma, dma, dma,
                 dma((nz,)), dma((nz,)), dma((nz, flat)), dma((nz, flat)), dma((nz,)), dma((nz,)),
             ],
             compiler_params=pltpu.CompilerParams(

time: 66.4 us -> 63.3 us (0.953)
  Pallas kernels: 62.1 us -> 59 us
    pallas_call x1, Pallas kernels: 62.1 us -> 59 us  [body(): pl.pallas_call(functools.partial(kernel, (ny, nz, nx), scale, hold), out_...]
where the time goes in v3:
time: 63.3 us; the launch traced here: 63 us
  Pallas kernels  59 us (93%)
  between operations  2.46 us (4%)
  other arithmetic  1.54 us (2%)
    pallas_call x1, Pallas kernels, body(): pl.pallas_call(functools.partial(kernel, (ny, nz, nx), scale, hold), out_...  59 us
    mul x1, other arithmetic, body(): return (mean[0, 0], grads * scale)  1.54 us

profile of v3, /device:TPU:0, one launch (start us, length us, event | category | flops | bytes accessed | tf_op | source)
XLA Modules:
  0.0 63.0 jit_solution(9000940630253774044)
XLA Ops:
  0.6 59.0 %retriever_step.1 = (f32[32,768]{1,0:T(8,128)}, f32[1,1]{1,0:T(1,128)}) custom-call(bf16[32,768]{1,0:T(8,128)(2,1)} %q_hbm.1, bf16[2048,768]{1,0:T(8,128)(2,1)} %p_hbm.1, s32[32,32]{1,0:T(8,128)} %id_hbm.1, f32[32,32]{1,0:T(8,128)} %reader_hbm.1), custom_call_target="tpu_custom_call" | custom-call | tf_op jit(solution)/shard_map/retriever_step/pallas_call | solution.py:402
  59.6 1.5 %broadcast_multiply_fusion = f32[32,768]{1,0:T(8,128)} fusion(f32[32,768]{1,0:T(8,128)} %get-tuple-element.5), kind=kLoop, calls=%fused_computation | loop fusion | flops 24576 | bytes 196608 | tf_op jit(solution)/shard_map/mul | solution.py:434

commit v4 on v3

v4 whole, which is shorter than its diff:
```python
import functools
import math

import jax
import jax.numpy as jnp
from jax import lax
from jax.experimental import pallas as pl
from jax.experimental.pallas import tpu as pltpu
from jax.sharding import PartitionSpec as P

MESH = pl.DeviceIdType.MESH
LANES = 128
SUB = 8
VMEM_LIMIT = 58 * 1024 * 1024


class Place:
    def __init__(self, sizes):
        self.ny, self.nz, self.nx = sizes
        self.flat = self.ny * self.nx
        self.chunk = 2 * self.flat
        self.n = self.chunk * self.nz
        index, bulk = lax.axis_index("index"), lax.axis_index("bulk")
        self.y, self.c = index // 2, index % 2
        self.z, self.x = bulk // self.nx, bulk % self.nx
        self.me = self.position(self.z, self.c, self.y, self.x)
        self.owner = index * self.nz * self.nx + bulk

    def position(self, z, c, y, x):
        return (z * 2 + c) * self.flat + y * self.nx + x

    def device(self, z, c, y, x):
        return (y * 2 + c, z * self.nx + x)

    def others(self, act):
        def one_plane(i, carry):
            z = lax.rem(self.z + i, self.nz)
            for c in (self.c, 1 - self.c):
                for a in range(self.ny):
                    for b in range(self.nx):
                        y, x = lax.rem(self.y + a, self.ny), lax.rem(self.x + b, self.nx)
                        if c is self.c and a == 0 and b == 0:
                            @pl.when(i > 0)
                            def _():
                                act(self.device(z, c, y, x))
                        else:
                            act(self.device(z, c, y, x))
            return carry

        lax.fori_loop(0, self.nz, one_plane, 0)

    def plane(self):
        for a in range(self.ny):
            for b in range(self.nx):
                if a or b:
                    yield (a * self.nx + b, (self.y + a) % self.ny, (self.x + b) % self.nx)


def wait_bytes(ref, sem):
    pltpu.make_async_copy(ref, ref, sem).wait()


def grouped(x, k, reduce, empty):
    group = lax.broadcasted_iota(jnp.int32, x.shape, 1) // k
    result = jnp.full(x.shape, empty, x.dtype)
    for j in range(x.shape[1] // k):
        value = reduce(jnp.where(group == j, x, empty), axis=1, keepdims=True)
        result = jnp.where(group == j, value, result)
    return result


def log_normalize(x, k):
    shifted = x - grouped(x, k, jnp.max, -jnp.inf)
    return shifted - jnp.log(grouped(jnp.exp(shifted), k, jnp.sum, 0.0))


def kernel(sizes, scale, cap, q_hbm, p_hbm, id_hbm, reader_hbm, out, mean,
           p_ref, id_ref, reader_ref, qall, idall, rank, found, held, ps, srecv, mine, mall, g, sib, acc, going, coming, zin,
           p_sem, in_sem, q_send, q_recv, id_send, id_recv, s_send, s_recv, w_send, w_recv,
           sib_send, sib_recv, p_send, p_recv, z_send, z_recv):
    t = Place(sizes)
    rows, k = id_ref.shape
    per, width = p_ref.shape
    tiles, group = per // LANES, LANES // k
    r8 = rows // group
    half = t.flat * rows
    f32, bf16 = jnp.float32, jnp.bfloat16

    def span(number, count):
        return pl.ds(pl.multiple_of(number * count, count), count)

    mine_in = [
        pltpu.make_async_copy(id_hbm, id_ref, in_sem.at[0]),
        pltpu.make_async_copy(reader_hbm, reader_ref, in_sem.at[1]),
        pltpu.make_async_copy(q_hbm, qall.at[span(t.me, rows)], in_sem.at[2]),
    ]
    for copy in mine_in:
        copy.start()
    load = pltpu.make_async_copy(p_hbm, p_ref, p_sem)
    load.start()
    barrier = pltpu.get_barrier_semaphore()

    t.others(lambda device: pl.semaphore_signal(
        barrier, inc=1, device_id=device, device_id_type=MESH))

    def packed(ref):
        return jnp.concatenate([ref[j * r8:(j + 1) * r8, :] for j in range(group)], axis=1)

    for copy in mine_in:
        copy.wait()
    idall[span(t.me, r8), :] = packed(id_ref)
    log_reader = log_normalize(packed(reader_ref), k)
    reader_prob = jnp.exp(log_reader)
    pl.semaphore_wait(barrier, t.n - 1)

    def to_all(src, dst, send_sem, recv_sem):
        t.others(lambda device: pltpu.make_async_remote_copy(
            src_ref=src, dst_ref=dst, send_sem=send_sem, recv_sem=recv_sem,
            device_id=device, device_id_type=MESH).start())

    def block(position):
        return qall.at[span(position, rows)]

    def give(src, position, device):
        pltpu.make_async_remote_copy(
            src_ref=src, dst_ref=block(position), send_sem=q_send, recv_sem=q_recv.at[position],
            device_id=device, device_id_type=MESH,
        ).start()

    def arrived(position):
        wait_bytes(block(position), q_recv.at[position])

    sibling = t.device(t.z, 1 - t.c, t.y, t.x)
    for i in range(1, t.nz):
        give(block(t.me), t.me, t.device((t.z + i) % t.nz, t.c, t.y, t.x))
    for _, y, x in t.plane():
        give(block(t.me), t.me, t.device(t.z, t.c, y, x))
    give(block(t.me), t.me, sibling)
    to_all(idall.at[span(t.me, r8)], idall.at[span(t.me, r8)], id_send, id_recv)

    for i in range(1, t.nz):
        position = t.position((t.z + i) % t.nz, t.c, t.y, t.x)
        arrived(position)
        for _, y, x in t.plane():
            give(block(position), position, t.device(t.z, t.c, y, x))
        give(block(position), position, sibling)

    def pass_plane(z):
        for _, y, x in t.plane():
            position = t.position(z, t.c, y, x)
            arrived(position)
            give(block(position), position, sibling)

    wait_bytes(idall.at[pl.ds(0, (t.n - 1) * r8)], id_recv)

    def iota(shape, dim):
        return lax.broadcasted_iota(jnp.int32, shape, dim)

    lane_group = iota((r8, LANES), 1) // k
    slots = iota((cap, LANES), 0).astype(f32)
    lanes = iota((cap, LANES), 1).astype(f32)
    count = SUB * r8
    before = (iota((LANES, LANES), 0) < iota((LANES, LANES), 1)).astype(f32).astype(bf16)
    row, col = iota((count, count), 0), iota((count, count), 1)
    above = ((row // r8 == col // r8) & (col < row)).astype(f32).astype(bf16)

    def one_rank(u, carry):
        at = pl.ds(pl.multiple_of(u * count, count), count)
        local = idall[at, :] - t.owner * per
        own = (local >= 0) & (local < per)
        ones = own.astype(f32).astype(bf16)
        earlier = jnp.dot(ones, before, preferred_element_type=f32)
        rows_above = jnp.sum(jnp.dot(above, ones, preferred_element_type=f32), axis=1, keepdims=True)
        rank[at, :] = jnp.where(own, earlier + rows_above, -1.0)
        return carry

    lax.fori_loop(0, t.n // SUB, one_rank, 0)
    load.wait()
    held[t.n * cap:, :] = jnp.zeros((LANES, width), bf16)

    def fetch(z):
        def one_sub(u, carry):
            first = z * t.chunk + u * SUB
            for v in range(SUB):
                at = span(first + v, r8)
                spot = rank[at, :]
                value = (idall[at, :] - t.owner * per + 1).astype(f32)
                chosen = jnp.zeros((cap, LANES), f32)
                for b in range(r8):
                    chosen = jnp.where(slots == spot[b:b + 1, :], value[b:b + 1, :], chosen)
                wanted = jnp.sum(chosen, axis=1, keepdims=True) - 1.0
                for h in range(tiles):
                    found[v * cap:(v + 1) * cap, h * LANES:(h + 1) * LANES] = jnp.where(
                        lanes == wanted - float(h * LANES), 1.0, 0.0).astype(bf16)
            held[pl.ds(pl.multiple_of(first * cap, SUB * cap), SUB * cap), :] = jnp.dot(
                found[...], p_ref[...], preferred_element_type=f32).astype(bf16)
            return carry

        lax.fori_loop(0, t.chunk // SUB, one_sub, 0)

    def score(z):
        def one_sub(u, carry):
            first = z * t.chunk + u * SUB
            for v in range(SUB):
                position = first + v
                products = lax.dot_general(
                    qall[span(position, rows), :], held[pl.ds(pl.multiple_of(position * cap, cap), LANES), :],
                    (((1,), (1,)), ((), ())), preferred_element_type=f32)
                spot = rank[span(position, r8), :].astype(jnp.int32)
                at = jnp.maximum(spot, 0)
                total = jnp.zeros((r8, LANES), f32)
                for j in range(group):
                    picked = jnp.take_along_axis(products[j * r8:(j + 1) * r8, :], at, axis=1)
                    total = jnp.where((spot >= 0) & (lane_group == j), picked, total)
                ps[span(position, r8), :] = total
            return carry

        lax.fori_loop(0, t.chunk // SUB, one_sub, 0)
        for c in range(2):
            for y in range(t.ny):
                for x in range(t.nx):
                    position = t.position(z, c, y, x)

                    @pl.when(position != t.me)
                    def _():
                        pltpu.make_async_remote_copy(
                            src_ref=ps.at[span(position, r8)], dst_ref=srecv.at[span(t.me, r8)],
                            send_sem=s_send, recv_sem=s_recv,
                            device_id=t.device(z, c, y, x), device_id_type=MESH,
                        ).start()

    def weigh():
        srecv[span(t.me, r8), :] = ps[span(t.me, r8), :]
        wait_bytes(srecv.at[pl.ds(0, (t.n - 1) * r8)], s_recv)
        scores = jnp.sum(srecv[...].reshape(t.n, r8, LANES), axis=0) * scale
        log_retriever = log_normalize(scores, k)
        weights = (jnp.exp(log_retriever) - reader_prob).astype(bf16).astype(f32)
        mine[0:r8, :] = weights
        mine[r8:2 * r8, :] = reader_prob * (log_reader - log_retriever)
        to_all(mine, mall.at[span(t.me, 2 * r8)], w_send, w_recv.at[t.z])
        mall[span(t.me, 2 * r8), :] = mine[...]

    def one_plane(step, carry):
        @pl.when(step < t.nz)
        def _():
            pass_plane(step)
            fetch(step)

            arrived(t.position(step, 1 - t.c, t.y, t.x))
            for _, y, x in t.plane():
                arrived(t.position(step, 1 - t.c, y, x))
            score(step)

        @pl.when(step == t.z + 2)
        def _():
            weigh()

        return carry

    lax.fori_loop(0, t.nz + 2, one_plane, 0)

    at_row = iota((rows, r8 * LANES), 1)
    pick = (iota((rows, r8 * LANES), 0) == at_row % LANES // k * r8 + at_row // LANES).astype(f32).astype(bf16)

    def grads(i):
        z = lax.rem(t.z + i, t.nz)
        weights_of = lambda count: wait_bytes(
            mall.at[pl.ds(pl.multiple_of(z * t.chunk * 2 * r8, 2 * r8), count * 2 * r8)], w_recv.at[z])

        @pl.when(i != 0)
        def _():
            weights_of(t.chunk)

        @pl.when(i == 0)
        def _():
            weights_of(t.chunk - 1)

        def one_sub(u, carry):
            for v in range(SUB):
                position = z * t.chunk + u * SUB + v
                spot = rank[span(position, r8), :]
                w = mall[pl.ds(pl.multiple_of(position * 2 * r8, 2 * r8), r8), :]
                spread = jnp.concatenate(
                    [jnp.where(slots == spot[b:b + 1, :], w[b:b + 1, :], 0.0).astype(bf16) for b in range(r8)],
                    axis=1)
                by_slot = lax.dot_general(
                    pick, spread, (((1,), (1,)), ((), ())), preferred_element_type=f32).astype(bf16)
                g[i, pl.ds(pl.multiple_of((u * SUB + v) * rows, rows), rows), :] = jnp.dot(
                    by_slot, held[pl.ds(pl.multiple_of(position * cap, cap), cap), :],
                    preferred_element_type=f32)
            return carry

        lax.fori_loop(0, t.chunk // SUB, one_sub, 0)
        first(i).start()

    def first(i):
        return pltpu.make_async_remote_copy(
            src_ref=g.at[i, span(1 - t.c, half)], dst_ref=sib.at[i],
            send_sem=sib_send.at[i], recv_sem=sib_recv.at[i],
            device_id=sibling, device_id_type=MESH)

    def second(i, o, y, x):
        return pltpu.make_async_remote_copy(
            src_ref=going.at[i, o], dst_ref=coming.at[i, o],
            send_sem=p_send.at[i, o], recv_sem=p_recv.at[i, o],
            device_id=t.device(t.z, t.c, y, x), device_id_type=MESH)

    def third(i):
        return pltpu.make_async_remote_copy(
            src_ref=acc.at[i], dst_ref=zin.at[i],
            send_sem=z_send.at[i], recv_sem=z_recv.at[i],
            device_id=t.device(lax.rem(t.z + i, t.nz), t.c, t.y, t.x), device_id_type=MESH)

    def summed(i, y, x):
        number = y * t.nx + x
        return (g[i, pl.ds(pl.multiple_of(t.c * half + number * rows, rows), rows), :]
                + sib[i, span(number, rows), :])

    def in_plane(i):
        first(i).wait_recv()
        for o, y, x in t.plane():
            going[i, o] = summed(i, y, x).astype(bf16)
            second(i, o, y, x).start()
        acc[i] = summed(i, t.y, t.x)

    def along_z(i):
        total = acc[i]
        for o, y, x in t.plane():
            second(i, o, y, x).wait_recv()
            total = total + coming[i, o].astype(f32)
        acc[i] = total

    def turn(step):
        z = step + (step >= t.z).astype(jnp.int32)
        return jnp.where(step >= t.nz - 1, 0, lax.rem(z - t.z + t.nz, t.nz))

    def one_step(step, carry):
        grads(turn(step))

        @pl.when(step >= 1)
        def _():
            in_plane(turn(step - 1))

        @pl.when(step >= 2)
        def _():
            along_z(turn(step - 2))
            third(turn(step - 2)).start()

        return carry

    lax.fori_loop(0, t.nz, one_step, 0)
    in_plane(0)
    last = turn(jnp.int32(t.nz - 2))
    along_z(last)
    third(last).start()
    divergence = mall[...].reshape(t.n, 2 * r8, LANES)[:, r8:, :]
    mean[0, 0] = jnp.sum(jnp.sum(divergence, axis=0)) / (t.n * rows)
    along_z(0)
    total = acc[0]
    for i in range(1, t.nz):
        third(i).wait_recv()
        total = total + zin[i]
    out[...] = total

    wait_bytes(qall.at[pl.ds(0, (t.n - 1) * rows)], q_send)
    wait_bytes(idall.at[pl.ds(0, (t.n - 1) * r8)], id_send)
    wait_bytes(srecv.at[pl.ds(0, (t.n - 1) * r8)], s_send)
    wait_bytes(mall.at[pl.ds(0, (t.n - 1) * 2 * r8)], w_send)
    for i in range(t.nz):
        first(i).wait_send()
        for o, y, x in t.plane():
            second(i, o, y, x).wait_send()
        if i:
            third(i).wait_send()


def solution(mesh):
    n_index, n_bulk = mesh.shape["index"], mesh.shape["bulk"]
    ny = n_index // 2
    nx = math.gcd(ny, n_bulk)
    nz = n_bulk // nx
    flat = ny * nx
    n = n_index * n_bulk
    vmem = pl.BlockSpec(memory_space=pltpu.VMEM)
    dma = pltpu.SemaphoreType.DMA

    def body(questions, passages, candidate_ids, reader_loglik):
        rows, k = candidate_ids.shape
        per, width = passages.shape
        r8 = rows * k // LANES
        scale = 4.0 / math.sqrt(width)
        f32, bf16, i32 = jnp.float32, jnp.bfloat16, jnp.int32
        cap = 2 * rows * k // n
        grads, mean = pl.pallas_call(
            functools.partial(kernel, (ny, nz, nx), scale, cap),
            out_shape=(jax.ShapeDtypeStruct((rows, width), f32), jax.ShapeDtypeStruct((1, 1), f32)),
            in_specs=[pl.BlockSpec(memory_space=pl.ANY)] * 4,
            out_specs=(vmem, pl.BlockSpec(memory_space=pltpu.SMEM)),
            scratch_shapes=[
                pltpu.VMEM((per, width), bf16),
                pltpu.VMEM((rows, k), i32),
                pltpu.VMEM((rows, k), f32),
                pltpu.VMEM((n * rows, width), bf16),
                pltpu.VMEM((n * r8, LANES), i32),
                pltpu.VMEM((n * r8, LANES), f32),
                pltpu.VMEM((SUB * cap, per), bf16),
                pltpu.VMEM((n * cap + LANES, width), bf16),
                pltpu.VMEM((n * r8, LANES), f32),
                pltpu.VMEM((n * r8, LANES), f32),
                pltpu.VMEM((2 * r8, LANES), f32),
                pltpu.VMEM((n * 2 * r8, LANES), f32),
                pltpu.VMEM((nz, 2 * flat * rows, width), f32),
                pltpu.VMEM((nz, flat * rows, width), f32),
                pltpu.VMEM((nz, rows, width), f32),
                pltpu.VMEM((nz, flat, rows, width), bf16),
                pltpu.VMEM((nz, flat, rows, width), bf16),
                pltpu.VMEM((nz, rows, width), f32),
                dma, dma((3,)), dma, dma((n,)), dma, dma, dma, dma, dma, dma((nz,)),
                dma((nz,)), dma((nz,)), dma((nz, flat)), dma((nz, flat)), dma((nz,)), dma((nz,)),
            ],
            compiler_params=pltpu.CompilerParams(
                collective_id=0, has_side_effects=True, vmem_limit_bytes=VMEM_LIMIT),
            name="retriever_step",
        )(questions, passages, candidate_ids, reader_loglik)
        return mean[0, 0], grads * scale

    placed = P(("index", "bulk"), None)
    return jax.shard_map(
        body, mesh=mesh, in_specs=(placed,) * 4, out_specs=(P(), placed), check_vma=False)
```

time: 63.3 us -> 67.4 us (1.065)
  the two profiles are of different devices: /device:TPU:0 before, /device:TPU:25 now
where the time goes in v4:
time: 67.4 us; the launch traced here: 67.2 us
  Pallas kernels  63.1 us (94%)
  between operations  2.46 us (4%)
  other arithmetic  1.54 us (2%)
    pallas_call x1, Pallas kernels, body(): pl.pallas_call(functools.partial(kernel, (ny, nz, nx), scale, cap), out_s...  63.1 us
    mul x1, other arithmetic, body(): return (mean[0, 0], grads * scale)  1.54 us

profile of v4, /device:TPU:25, one launch (start us, length us, event | category | flops | bytes accessed | tf_op | source)
XLA Modules:
  0.0 67.2 jit_solution(13519201593593480286)
XLA Ops:
  0.6 63.1 %retriever_step.1 = (f32[32,768]{1,0:T(8,128)}, f32[1,1]{1,0:T(1,128)}) custom-call(bf16[32,768]{1,0:T(8,128)(2,1)} %q_hbm.1, bf16[2048,768]{1,0:T(8,128)(2,1)} %p_hbm.1, s32[32,32]{1,0:T(8,128)} %id_hbm.1, f32[32,32]{1,0:T(8,128)} %reader_hbm.1), custom_call_target="tpu_custom_call" | custom-call | tf_op jit(solution)/shard_map/retriever_step/pallas_call | solution.py:394
  63.8 1.5 %broadcast_multiply_fusion = f32[32,768]{1,0:T(8,128)} fusion(f32[32,768]{1,0:T(8,128)} %get-tuple-element.5), kind=kLoop, calls=%fused_computation | loop fusion | flops 24576 | bytes 196608 | tf_op jit(solution)/shard_map/mul | solution.py:425

commit v5 on v4

--- a/solution.py
+++ b/solution.py
@@ -24,6 +24,7 @@
         self.y, self.c = index // 2, index % 2
         self.z, self.x = bulk // self.nx, bulk % self.nx
         self.me = self.position(self.z, self.c, self.y, self.x)
+        self.mine = self.small(self.z, self.c, self.y, self.x)
         self.owner = index * self.nz * self.nx + bulk
 
     def position(self, z, c, y, x):
@@ -32,22 +33,8 @@
     def device(self, z, c, y, x):
         return (y * 2 + c, z * self.nx + x)
 
-    def others(self, act):
-        def one_plane(i, carry):
-            z = lax.rem(self.z + i, self.nz)
-            for c in (self.c, 1 - self.c):
-                for a in range(self.ny):
-                    for b in range(self.nx):
-                        y, x = lax.rem(self.y + a, self.ny), lax.rem(self.x + b, self.nx)
-                        if c is self.c and a == 0 and b == 0:
-                            @pl.when(i > 0)
-                            def _():
-                                act(self.device(z, c, y, x))
-                        else:
-                            act(self.device(z, c, y, x))
-            return carry
-
-        lax.fori_loop(0, self.nz, one_plane, 0)
+    def small(self, z, c, y, x):
+        return ((c * self.ny + y) * self.nx + x) * self.nz + z
 
     def plane(self):
         for a in range(self.ny):
@@ -75,8 +62,9 @@
 
 
 def kernel(sizes, scale, cap, q_hbm, p_hbm, id_hbm, reader_hbm, out, mean,
-           p_ref, id_ref, reader_ref, qall, idall, rank, found, held, ps, srecv, mine, mall, g, sib, acc, going, coming, zin,
-           p_sem, in_sem, q_send, q_recv, id_send, id_recv, s_send, s_recv, w_send, w_recv,
+           p_ref, id_ref, reader_ref, qall, idall, rank, found, held, ps, s1, s2, s2out, s3, mall, g, sib, acc, going, coming, zin,
+           p_sem, in_sem, q_send, q_recv, q_sib, id_send, id_z, id_plane, id_sib,
+           s_send, s_recv, w_send, w_z, w_plane, w_sib,
            sib_send, sib_recv, p_send, p_recv, z_send, z_recv):
     t = Place(sizes)
     rows, k = id_ref.shape
@@ -85,6 +73,7 @@
     r8 = rows // group
     half = t.flat * rows
     f32, bf16 = jnp.float32, jnp.bfloat16
+    id_sems, w_sems = (id_send, id_z, id_plane, id_sib), (w_send, w_z, w_plane, w_sib)
 
     def span(number, count):
         return pl.ds(pl.multiple_of(number * count, count), count)
@@ -100,23 +89,51 @@
     load.start()
     barrier = pltpu.get_barrier_semaphore()
 
-    t.others(lambda device: pl.semaphore_signal(
-        barrier, inc=1, device_id=device, device_id_type=MESH))
+    sibling = t.device(t.z, 1 - t.c, t.y, t.x)
+    column = [(i, t.device((t.z + i) % t.nz, t.c, t.y, t.x)) for i in range(1, t.nz)]
+    around = [(o, t.device(t.z, t.c, y, x)) for o, y, x in t.plane()]
+    near = [sibling] + [device for _, device in column + around]
+    for device in near:
+        pl.semaphore_signal(barrier, inc=1, device_id=device, device_id_type=MESH)
 
     def packed(ref):
         return jnp.concatenate([ref[j * r8:(j + 1) * r8, :] for j in range(group)], axis=1)
 
     for copy in mine_in:
         copy.wait()
-    idall[span(t.me, r8), :] = packed(id_ref)
+    idall[span(t.mine, r8), :] = packed(id_ref)
     log_reader = log_normalize(packed(reader_ref), k)
     reader_prob = jnp.exp(log_reader)
-    pl.semaphore_wait(barrier, t.n - 1)
-
-    def to_all(src, dst, send_sem, recv_sem):
-        t.others(lambda device: pltpu.make_async_remote_copy(
+    pl.semaphore_wait(barrier, len(near))
+
+    def send(src, dst, send_sem, recv_sem, device):
+        copy = pltpu.make_async_remote_copy(
             src_ref=src, dst_ref=dst, send_sem=send_sem, recv_sem=recv_sem,
-            device_id=device, device_id_type=MESH).start())
+            device_id=device, device_id_type=MESH)
+        copy.start()
+
+    def share_z(ref, count, sems):
+        at = ref.at[span(t.mine, count)]
+        for i, device in column:
+            send(at, at, sems[0], sems[1].at[i], device)
+
+    def share_plane(ref, count, sems):
+        for i in range(1, t.nz):
+            z = (t.z - i + t.nz) % t.nz
+            wait_bytes(ref.at[span(t.small(z, t.c, t.y, t.x), count)], sems[1].at[i])
+        at = ref.at[span(t.mine // t.nz, t.nz * count)]
+        for o, device in around:
+            send(at, at, sems[0], sems[2].at[o], device)
+
+    def share_sibling(ref, count, sems):
+        for o, y, x in t.plane():
+            y, x = (2 * t.y - y + t.ny) % t.ny, (2 * t.x - x + t.nx) % t.nx
+            wait_bytes(ref.at[span(t.small(0, t.c, y, x) // t.nz, t.nz * count)], sems[2].at[o])
+        at = ref.at[span(t.c, t.flat * t.nz * count)]
+        send(at, at, sems[0], sems[3], sibling)
+
+    def share_done(ref, count, sems):
+        wait_bytes(ref.at[span(1 - t.c, t.flat * t.nz * count)], sems[3])
 
     def block(position):
         return qall.at[span(position, rows)]
@@ -130,28 +147,27 @@
     def arrived(position):
         wait_bytes(block(position), q_recv.at[position])
 
-    sibling = t.device(t.z, 1 - t.c, t.y, t.x)
-    for i in range(1, t.nz):
-        give(block(t.me), t.me, t.device((t.z + i) % t.nz, t.c, t.y, t.x))
-    for _, y, x in t.plane():
-        give(block(t.me), t.me, t.device(t.z, t.c, y, x))
-    give(block(t.me), t.me, sibling)
-    to_all(idall.at[span(t.me, r8)], idall.at[span(t.me, r8)], id_send, id_recv)
-
+    share_z(idall, r8, id_sems)
+    for _, device in column + around:
+        give(block(t.me), t.me, device)
+    share_plane(idall, r8, id_sems)
     for i in range(1, t.nz):
         position = t.position((t.z + i) % t.nz, t.c, t.y, t.x)
         arrived(position)
-        for _, y, x in t.plane():
-            give(block(position), position, t.device(t.z, t.c, y, x))
-        give(block(position), position, sibling)
+        for _, device in around:
+            give(block(position), position, device)
+    share_sibling(idall, r8, id_sems)
+
+    def side(z, c):
+        return qall.at[span(z * 2 + c, half)]
 
     def pass_plane(z):
         for _, y, x in t.plane():
-            position = t.position(z, t.c, y, x)
-            arrived(position)
-            give(block(position), position, sibling)
-
-    wait_bytes(idall.at[pl.ds(0, (t.n - 1) * r8)], id_recv)
+            arrived(t.position(z, t.c, y, x))
+        send(side(z, t.c), side(z, t.c), q_send, q_sib.at[z], sibling)
+
+    pass_plane(t.z)
+    share_done(idall, r8, id_sems)
 
     def iota(shape, dim):
         return lax.broadcasted_iota(jnp.int32, shape, dim)
@@ -182,16 +198,20 @@
         def one_sub(u, carry):
             first = z * t.chunk + u * SUB
             for v in range(SUB):
-                at = span(first + v, r8)
+                at = span((u * SUB + v) * t.nz + z, r8)
                 spot = rank[at, :]
                 value = (idall[at, :] - t.owner * per + 1).astype(f32)
                 chosen = jnp.zeros((cap, LANES), f32)
                 for b in range(r8):
                     chosen = jnp.where(slots == spot[b:b + 1, :], value[b:b + 1, :], chosen)
                 wanted = jnp.sum(chosen, axis=1, keepdims=True) - 1.0
+                wanted = jnp.broadcast_to(wanted, (cap, LANES))
+                high = jnp.floor(wanted * (1.0 / LANES))
+                low_hot = jnp.where(lanes == wanted - high * LANES, 1.0, 0.0).astype(bf16)
+                high = high.astype(bf16)
                 for h in range(tiles):
                     found[v * cap:(v + 1) * cap, h * LANES:(h + 1) * LANES] = jnp.where(
-                        lanes == wanted - float(h * LANES), 1.0, 0.0).astype(bf16)
+                        high == jnp.full((cap, LANES), h, bf16), low_hot, jnp.zeros_like(low_hot))
             held[pl.ds(pl.multiple_of(first * cap, SUB * cap), SUB * cap), :] = jnp.dot(
                 found[...], p_ref[...], preferred_element_type=f32).astype(bf16)
             return carry
@@ -206,80 +226,81 @@
                 products = lax.dot_general(
                     qall[span(position, rows), :], held[pl.ds(pl.multiple_of(position * cap, cap), LANES), :],
                     (((1,), (1,)), ((), ())), preferred_element_type=f32)
-                spot = rank[span(position, r8), :].astype(jnp.int32)
+                small = (u * SUB + v) * t.nz + z
+                spot = rank[span(small, r8), :].astype(jnp.int32)
                 at = jnp.maximum(spot, 0)
                 total = jnp.zeros((r8, LANES), f32)
                 for j in range(group):
                     picked = jnp.take_along_axis(products[j * r8:(j + 1) * r8, :], at, axis=1)
                     total = jnp.where((spot >= 0) & (lane_group == j), picked, total)
-                ps[span(position, r8), :] = total
+                ps[span(small, r8), :] = total
             return carry
 
         lax.fori_loop(0, t.chunk // SUB, one_sub, 0)
-        for c in range(2):
-            for y in range(t.ny):
-                for x in range(t.nx):
-                    position = t.position(z, c, y, x)
-
-                    @pl.when(position != t.me)
-                    def _():
-                        pltpu.make_async_remote_copy(
-                            src_ref=ps.at[span(position, r8)], dst_ref=srecv.at[span(t.me, r8)],
-                            send_sem=s_send, recv_sem=s_recv,
-                            device_id=t.device(z, c, y, x), device_id_type=MESH,
-                        ).start()
-
-    def weigh():
-        srecv[span(t.me, r8), :] = ps[span(t.me, r8), :]
-        wait_bytes(srecv.at[pl.ds(0, (t.n - 1) * r8)], s_recv)
-        scores = jnp.sum(srecv[...].reshape(t.n, r8, LANES), axis=0) * scale
-        log_retriever = log_normalize(scores, k)
-        weights = (jnp.exp(log_retriever) - reader_prob).astype(bf16).astype(f32)
-        mine[0:r8, :] = weights
-        mine[r8:2 * r8, :] = reader_prob * (log_reader - log_retriever)
-        to_all(mine, mall.at[span(t.me, 2 * r8)], w_send, w_recv.at[t.z])
-        mall[span(t.me, 2 * r8), :] = mine[...]
-
-    def one_plane(step, carry):
-        @pl.when(step < t.nz)
+    def one_fetch(i, carry):
+        z = lax.rem(t.z + i, t.nz)
+
+        @pl.when(i > 0)
         def _():
-            pass_plane(step)
-            fetch(step)
-
-            arrived(t.position(step, 1 - t.c, t.y, t.x))
-            for _, y, x in t.plane():
-                arrived(t.position(step, 1 - t.c, y, x))
-            score(step)
-
-        @pl.when(step == t.z + 2)
-        def _():
-            weigh()
-
+            pass_plane(z)
+
+        fetch(z)
         return carry
 
-    lax.fori_loop(0, t.nz + 2, one_plane, 0)
+    def one_score(i, carry):
+        z = lax.rem(t.z + i, t.nz)
+        wait_bytes(side(z, 1 - t.c), q_sib.at[z])
+        score(z)
+        return carry
+
+    lax.fori_loop(0, t.nz, one_fetch, 0)
+    lax.fori_loop(0, t.nz, one_score, 0)
+
+    column_rows = t.nz * r8
+    send(ps.at[span(1 - t.c, t.flat * column_rows)], s1, s_send.at[0], s_recv.at[0], sibling)
+    wait_bytes(s1, s_recv.at[0])
+
+    def score_part(y, x):
+        number = y * t.nx + x
+        return (ps[span(t.c * t.flat + number, column_rows), :] + s1[span(number, column_rows), :])
+
+    for o, y, x in t.plane():
+        s2out[o] = score_part(y, x)
+        send(s2out.at[o], s2.at[o], s_send.at[o], s_recv.at[o], t.device(t.z, t.c, y, x))
+    total = score_part(t.y, t.x)
+    for o, _ in around:
+        wait_bytes(s2.at[o], s_recv.at[o])
+        total = total + s2[o]
+    s2out[0] = total
+    for i, device in column:
+        send(s2out.at[0, span((t.z + i) % t.nz, r8)], s3.at[i], s_send.at[t.flat + i], s_recv.at[t.flat + i], device)
+    scores = s2out[0, span(t.z, r8), :]
+    for i, _ in column:
+        wait_bytes(s3.at[i], s_recv.at[t.flat + i])
+        scores = scores + s3[i]
+
+    log_retriever = log_normalize(scores * scale, k)
+    weights = (jnp.exp(log_retriever) - reader_prob).astype(bf16).astype(f32)
+    both = 2 * r8
+    mall[span(t.mine, both), :] = jnp.concatenate(
+        [weights, reader_prob * (log_reader - log_retriever)], axis=0)
+    share_z(mall, both, w_sems)
+    share_plane(mall, both, w_sems)
+    share_sibling(mall, both, w_sems)
+    share_done(mall, both, w_sems)
 
     at_row = iota((rows, r8 * LANES), 1)
     pick = (iota((rows, r8 * LANES), 0) == at_row % LANES // k * r8 + at_row // LANES).astype(f32).astype(bf16)
 
     def grads(i):
         z = lax.rem(t.z + i, t.nz)
-        weights_of = lambda count: wait_bytes(
-            mall.at[pl.ds(pl.multiple_of(z * t.chunk * 2 * r8, 2 * r8), count * 2 * r8)], w_recv.at[z])
-
-        @pl.when(i != 0)
-        def _():
-            weights_of(t.chunk)
-
-        @pl.when(i == 0)
-        def _():
-            weights_of(t.chunk - 1)
 
         def one_sub(u, carry):
             for v in range(SUB):
                 position = z * t.chunk + u * SUB + v
-                spot = rank[span(position, r8), :]
-                w = mall[pl.ds(pl.multiple_of(position * 2 * r8, 2 * r8), r8), :]
+                small = (u * SUB + v) * t.nz + z
+                spot = rank[span(small, r8), :]
+                w = mall[pl.ds(pl.multiple_of(small * 2 * r8, 2 * r8), r8), :]
                 spread = jnp.concatenate(
                     [jnp.where(slots == spot[b:b + 1, :], w[b:b + 1, :], 0.0).astype(bf16) for b in range(r8)],
                     axis=1)
@@ -331,8 +352,7 @@
         acc[i] = total
 
     def turn(step):
-        z = step + (step >= t.z).astype(jnp.int32)
-        return jnp.where(step >= t.nz - 1, 0, lax.rem(z - t.z + t.nz, t.nz))
+        return lax.rem(step + 1, t.nz)
 
     def one_step(step, carry):
         grads(turn(step))
@@ -350,9 +370,8 @@
 
     lax.fori_loop(0, t.nz, one_step, 0)
     in_plane(0)
-    last = turn(jnp.int32(t.nz - 2))
-    along_z(last)
-    third(last).start()
+    along_z(t.nz - 1)
+    third(t.nz - 1).start()
     divergence = mall[...].reshape(t.n, 2 * r8, LANES)[:, r8:, :]
     mean[0, 0] = jnp.sum(jnp.sum(divergence, axis=0)) / (t.n * rows)
     along_z(0)
@@ -363,9 +382,13 @@
     out[...] = total
 
     wait_bytes(qall.at[pl.ds(0, (t.n - 1) * rows)], q_send)
-    wait_bytes(idall.at[pl.ds(0, (t.n - 1) * r8)], id_send)
-    wait_bytes(srecv.at[pl.ds(0, (t.n - 1) * r8)], s_send)
-    wait_bytes(mall.at[pl.ds(0, (t.n - 1) * 2 * r8)], w_send)
+    wait_bytes(idall.at[pl.ds(0, (t.n - 1) * r8)], id_sems[0])
+    wait_bytes(mall.at[pl.ds(0, (t.n - 1) * both)], w_sems[0])
+    wait_bytes(s1, s_send.at[0])
+    for o, _ in around:
+        wait_bytes(s2.at[o], s_send.at[o])
+    for i, _ in column:
+        wait_bytes(s3.at[i], s_send.at[t.flat + i])
     for i in range(t.nz):
         first(i).wait_send()
         for o, y, x in t.plane():
@@ -406,8 +429,10 @@
                 pltpu.VMEM((SUB * cap, per), bf16),
                 pltpu.VMEM((n * cap + LANES, width), bf16),
                 pltpu.VMEM((n * r8, LANES), f32),
-                pltpu.VMEM((n * r8, LANES), f32),
-                pltpu.VMEM((2 * r8, LANES), f32),
+                pltpu.VMEM((n // 2 * r8, LANES), f32),
+                pltpu.VMEM((flat, nz * r8, LANES), f32),
+                pltpu.VMEM((flat, nz * r8, LANES), f32),
+                pltpu.VMEM((nz, r8, LANES), f32),
                 pltpu.VMEM((n * 2 * r8, LANES), f32),
                 pltpu.VMEM((nz, 2 * flat * rows, width), f32),
                 pltpu.VMEM((nz, flat * rows, width), f32),
@@ -415,7 +440,8 @@
                 pltpu.VMEM((nz, flat, rows, width), bf16),
                 pltpu.VMEM((nz, flat, rows, width), bf16),
                 pltpu.VMEM((nz, rows, width), f32),
-                dma, dma((3,)), dma, dma((n,)), dma, dma, dma, dma, dma, dma((nz,)),
+                dma, dma((3,)), dma, dma((n,)), dma((nz,)), dma, dma((nz,)), dma((flat,)), dma,
+                dma((flat + nz,)), dma((flat + nz,)), dma, dma((nz,)), dma((flat,)), dma,
                 dma((nz,)), dma((nz,)), dma((nz, flat)), dma((nz, flat)), dma((nz,)), dma((nz,)),
             ],
             compiler_params=pltpu.CompilerParams(

time: 67.4 us -> 67.6 us (level)
  the two profiles are of different devices: /device:TPU:25 before, /device:TPU:0 now
where the time goes in v5:
time: 67.6 us; the launch traced here: 67.3 us
  Pallas kernels  63.3 us (94%)
  between operations  2.46 us (4%)
  other arithmetic  1.54 us (2%)
    pallas_call x1, Pallas kernels, body(): pl.pallas_call(functools.partial(kernel, (ny, nz, nx), scale, cap), out_s...  63.3 us
    mul x1, other arithmetic, body(): return (mean[0, 0], grads * scale)  1.54 us

profile of v5, /device:TPU:0, one launch (start us, length us, event | category | flops | bytes accessed | tf_op | source)
XLA Modules:
  0.0 67.3 jit_solution(7735045264372276135)
XLA Ops:
  0.6 63.3 %retriever_step.1 = (f32[32,768]{1,0:T(8,128)}, f32[1,1]{1,0:T(1,128)}) custom-call(bf16[32,768]{1,0:T(8,128)(2,1)} %q_hbm.1, bf16[2048,768]{1,0:T(8,128)(2,1)} %p_hbm.1, s32[32,32]{1,0:T(8,128)} %id_hbm.1, f32[32,32]{1,0:T(8,128)} %reader_hbm.1), custom_call_target="tpu_custom_call" | custom-call | tf_op jit(solution)/shard_map/retriever_step/pallas_call | solution.py:417
  64.0 1.5 %broadcast_multiply_fusion = f32[32,768]{1,0:T(8,128)} fusion(f32[32,768]{1,0:T(8,128)} %get-tuple-element.5), kind=kLoop, calls=%fused_computation | loop fusion | flops 24576 | bytes 196608 | tf_op jit(solution)/shard_map/mul | solution.py:451

commit v6 on v4

--- a/solution.py
+++ b/solution.py
@@ -75,7 +75,7 @@
 
 
 def kernel(sizes, scale, cap, q_hbm, p_hbm, id_hbm, reader_hbm, out, mean,
-           p_ref, id_ref, reader_ref, qall, idall, rank, found, held, ps, srecv, mine, mall, g, sib, acc, going, coming, zin,
+           p_ref, id_ref, reader_ref, qall, idall, rank, s, found, held, ps, srecv, mine, mall, g, sib, acc, going, coming, zout, zin,
            p_sem, in_sem, q_send, q_recv, id_send, id_recv, s_send, s_recv, w_send, w_recv,
            sib_send, sib_recv, p_send, p_recv, z_send, z_recv):
     t = Place(sizes)
@@ -189,9 +189,13 @@
                 for b in range(r8):
                     chosen = jnp.where(slots == spot[b:b + 1, :], value[b:b + 1, :], chosen)
                 wanted = jnp.sum(chosen, axis=1, keepdims=True) - 1.0
+                wanted = jnp.broadcast_to(wanted, (cap, LANES))
+                high = jnp.floor(wanted * (1.0 / LANES))
+                low_hot = jnp.where(lanes == wanted - high * LANES, 1.0, 0.0).astype(bf16)
+                high = high.astype(bf16)
                 for h in range(tiles):
                     found[v * cap:(v + 1) * cap, h * LANES:(h + 1) * LANES] = jnp.where(
-                        lanes == wanted - float(h * LANES), 1.0, 0.0).astype(bf16)
+                        high == jnp.full((cap, LANES), h, bf16), low_hot, jnp.zeros_like(low_hot))
             held[pl.ds(pl.multiple_of(first * cap, SUB * cap), SUB * cap), :] = jnp.dot(
                 found[...], p_ref[...], preferred_element_type=f32).astype(bf16)
             return carry
@@ -201,18 +205,27 @@
     def score(z):
         def one_sub(u, carry):
             first = z * t.chunk + u * SUB
-            for v in range(SUB):
-                position = first + v
-                products = lax.dot_general(
-                    qall[span(position, rows), :], held[pl.ds(pl.multiple_of(position * cap, cap), LANES), :],
+            q = qall[pl.ds(pl.multiple_of(first * rows, SUB * rows), SUB * rows), :]
+            codes, lows, totals = [], [], [None] * SUB
+            for i in range(SUB):
+                local = idall[span(first + i, r8), :] - t.owner * per
+                own = (local >= 0) & (local < per)
+                codes.append(jnp.where(own, lane_group * tiles + local // LANES, -1))
+                lows.append(local & (LANES - 1))
+            for h in range(0, tiles, 2):
+                s[h // 2] = lax.dot_general(
+                    q, p_ref[h * LANES:(h + 2) * LANES, :],
                     (((1,), (1,)), ((), ())), preferred_element_type=f32)
-                spot = rank[span(position, r8), :].astype(jnp.int32)
-                at = jnp.maximum(spot, 0)
-                total = jnp.zeros((r8, LANES), f32)
-                for j in range(group):
-                    picked = jnp.take_along_axis(products[j * r8:(j + 1) * r8, :], at, axis=1)
-                    total = jnp.where((spot >= 0) & (lane_group == j), picked, total)
-                ps[span(position, r8), :] = total
+            for h in range(tiles):
+                for i in range(SUB):
+                    for j in range(group):
+                        piece = s[h // 2, i * rows + j * r8:i * rows + (j + 1) * r8,
+                                  h % 2 * LANES:(h % 2 + 1) * LANES]
+                        picked = jnp.take_along_axis(piece, lows[i], axis=1)
+                        picked = jnp.where(codes[i] == j * tiles + h, picked, 0.0)
+                        totals[i] = picked if totals[i] is None else totals[i] + picked
+            for i in range(SUB):
+                ps[span(first + i, r8), :] = totals[i]
             return carry
 
         lax.fori_loop(0, t.chunk // SUB, one_sub, 0)
@@ -240,24 +253,33 @@
         to_all(mine, mall.at[span(t.me, 2 * r8)], w_send, w_recv.at[t.z])
         mall[span(t.me, 2 * r8), :] = mine[...]
 
-    def one_plane(step, carry):
-        @pl.when(step < t.nz)
-        def _():
-            pass_plane(step)
-            fetch(step)
-
-            arrived(t.position(step, 1 - t.c, t.y, t.x))
-            for _, y, x in t.plane():
-                arrived(t.position(step, 1 - t.c, y, x))
-            score(step)
-
-        @pl.when(step == t.z + 2)
+    pass_plane(t.z)
+    fetch(t.z)
+
+    def one_plane(i, carry):
+        @pl.when(i + 1 < t.nz)
+        def _():
+            pass_plane(lax.rem(t.z + i + 1, t.nz))
+
+        z = lax.rem(t.z + i, t.nz)
+        arrived(t.position(z, 1 - t.c, t.y, t.x))
+        for _, y, x in t.plane():
+            arrived(t.position(z, 1 - t.c, y, x))
+        score(z)
+        return carry
+
+    lax.fori_loop(0, t.nz, one_plane, 0)
+
+    def one_fetch(i, carry):
+        fetch(lax.rem(t.z + i, t.nz))
+
+        @pl.when(i == 1)
         def _():
             weigh()
 
         return carry
 
-    lax.fori_loop(0, t.nz + 2, one_plane, 0)
+    lax.fori_loop(1, t.nz, one_fetch, 0)
 
     at_row = iota((rows, r8 * LANES), 1)
     pick = (iota((rows, r8 * LANES), 0) == at_row % LANES // k * r8 + at_row // LANES).astype(f32).astype(bf16)
@@ -307,7 +329,7 @@
 
     def third(i):
         return pltpu.make_async_remote_copy(
-            src_ref=acc.at[i], dst_ref=zin.at[i],
+            src_ref=zout.at[i], dst_ref=zin.at[i],
             send_sem=z_send.at[i], recv_sem=z_recv.at[i],
             device_id=t.device(lax.rem(t.z + i, t.nz), t.c, t.y, t.x), device_id_type=MESH)
 
@@ -329,10 +351,10 @@
             second(i, o, y, x).wait_recv()
             total = total + coming[i, o].astype(f32)
         acc[i] = total
+        zout[i] = total.astype(bf16)
 
     def turn(step):
-        z = step + (step >= t.z).astype(jnp.int32)
-        return jnp.where(step >= t.nz - 1, 0, lax.rem(z - t.z + t.nz, t.nz))
+        return lax.rem(step + 1, t.nz)
 
     def one_step(step, carry):
         grads(turn(step))
@@ -350,16 +372,15 @@
 
     lax.fori_loop(0, t.nz, one_step, 0)
     in_plane(0)
-    last = turn(jnp.int32(t.nz - 2))
-    along_z(last)
-    third(last).start()
+    along_z(t.nz - 1)
+    third(t.nz - 1).start()
     divergence = mall[...].reshape(t.n, 2 * r8, LANES)[:, r8:, :]
     mean[0, 0] = jnp.sum(jnp.sum(divergence, axis=0)) / (t.n * rows)
     along_z(0)
     total = acc[0]
     for i in range(1, t.nz):
         third(i).wait_recv()
-        total = total + zin[i]
+        total = total + zin[i].astype(f32)
     out[...] = total
 
     wait_bytes(qall.at[pl.ds(0, (t.n - 1) * rows)], q_send)
@@ -403,6 +424,7 @@
                 pltpu.VMEM((n * rows, width), bf16),
                 pltpu.VMEM((n * r8, LANES), i32),
                 pltpu.VMEM((n * r8, LANES), f32),
+                pltpu.VMEM((per // LANES // 2, SUB * rows, 2 * LANES), f32),
                 pltpu.VMEM((SUB * cap, per), bf16),
                 pltpu.VMEM((n * cap + LANES, width), bf16),
                 pltpu.VMEM((n * r8, LANES), f32),
@@ -414,7 +436,8 @@
                 pltpu.VMEM((nz, rows, width), f32),
                 pltpu.VMEM((nz, flat, rows, width), bf16),
                 pltpu.VMEM((nz, flat, rows, width), bf16),
-                pltpu.VMEM((nz, rows, width), f32),
+                pltpu.VMEM((nz, rows, width), bf16),
+                pltpu.VMEM((nz, rows, width), bf16),
                 dma, dma((3,)), dma, dma((n,)), dma, dma, dma, dma, dma, dma((nz,)),
                 dma((nz,)), dma((nz,)), dma((nz, flat)), dma((nz, flat)), dma((nz,)), dma((nz,)),
             ],

time: 67.4 us -> 59.5 us (0.88)
  the two profiles are of different devices: /device:TPU:25 before, /device:TPU:0 now
where the time goes in v6:
time: 59.5 us; the launch traced here: 59.2 us
  Pallas kernels  55.2 us (93%)
  between operations  2.46 us (4%)
  other arithmetic  1.54 us (3%)
    pallas_call x1, Pallas kernels, body(): pl.pallas_call(functools.partial(kernel, (ny, nz, nx), scale, cap), out_s...  55.2 us
    mul x1, other arithmetic, body(): return (mean[0, 0], grads * scale)  1.54 us

profile of v6, /device:TPU:0, one launch (start us, length us, event | category | flops | bytes accessed | tf_op | source)
XLA Modules:
  0.0 59.2 jit_solution(11665830086814444647)
XLA Ops:
  0.6 55.2 %retriever_step.1 = (f32[32,768]{1,0:T(8,128)}, f32[1,1]{1,0:T(1,128)}) custom-call(bf16[32,768]{1,0:T(8,128)(2,1)} %q_hbm.1, bf16[2048,768]{1,0:T(8,128)(2,1)} %p_hbm.1, s32[32,32]{1,0:T(8,128)} %id_hbm.1, f32[32,32]{1,0:T(8,128)} %reader_hbm.1), custom_call_target="tpu_custom_call" | custom-call | tf_op jit(solution)/shard_map/retriever_step/pallas_call | solution.py:415
  55.8 1.5 %broadcast_multiply_fusion = f32[32,768]{1,0:T(8,128)} fusion(f32[32,768]{1,0:T(8,128)} %get-tuple-element.5), kind=kLoop, calls=%fused_computation | loop fusion | flops 24576 | bytes 196608 | tf_op jit(solution)/shard_map/mul | solution.py:448

commit v7 on v6

--- a/solution.py
+++ b/solution.py
@@ -180,29 +180,34 @@
 
     def fetch(z):
         def one_sub(u, carry):
-            first = z * t.chunk + u * SUB
-            for v in range(SUB):
-                at = span(first + v, r8)
-                spot = rank[at, :]
-                value = (idall[at, :] - t.owner * per + 1).astype(f32)
-                chosen = jnp.zeros((cap, LANES), f32)
-                for b in range(r8):
-                    chosen = jnp.where(slots == spot[b:b + 1, :], value[b:b + 1, :], chosen)
-                wanted = jnp.sum(chosen, axis=1, keepdims=True) - 1.0
-                wanted = jnp.broadcast_to(wanted, (cap, LANES))
-                high = jnp.floor(wanted * (1.0 / LANES))
-                low_hot = jnp.where(lanes == wanted - high * LANES, 1.0, 0.0).astype(bf16)
-                high = high.astype(bf16)
-                for h in range(tiles):
-                    found[v * cap:(v + 1) * cap, h * LANES:(h + 1) * LANES] = jnp.where(
-                        high == jnp.full((cap, LANES), h, bf16), low_hot, jnp.zeros_like(low_hot))
-            held[pl.ds(pl.multiple_of(first * cap, SUB * cap), SUB * cap), :] = jnp.dot(
-                found[...], p_ref[...], preferred_element_type=f32).astype(bf16)
+            find(z * t.chunk + u * SUB)
+            hold(z * t.chunk + u * SUB)
             return carry
 
         lax.fori_loop(0, t.chunk // SUB, one_sub, 0)
 
-    def score(z):
+    def find(first):
+        for v in range(SUB):
+            at = span(first + v, r8)
+            spot = rank[at, :]
+            value = (idall[at, :] - t.owner * per + 1).astype(f32)
+            chosen = jnp.zeros((cap, LANES), f32)
+            for b in range(r8):
+                chosen = jnp.where(slots == spot[b:b + 1, :], value[b:b + 1, :], chosen)
+            wanted = jnp.sum(chosen, axis=1, keepdims=True) - 1.0
+            wanted = jnp.broadcast_to(wanted, (cap, LANES))
+            high = jnp.floor(wanted * (1.0 / LANES))
+            low_hot = jnp.where(lanes == wanted - high * LANES, 1.0, 0.0).astype(bf16)
+            high = high.astype(bf16)
+            for h in range(tiles):
+                found[v * cap:(v + 1) * cap, h * LANES:(h + 1) * LANES] = jnp.where(
+                    high == jnp.full((cap, LANES), h, bf16), low_hot, jnp.zeros_like(low_hot))
+
+    def hold(first):
+        held[pl.ds(pl.multiple_of(first * cap, SUB * cap), SUB * cap), :] = jnp.dot(
+            found[...], p_ref[...], preferred_element_type=f32).astype(bf16)
+
+    def score(z, fetching):
         def one_sub(u, carry):
             first = z * t.chunk + u * SUB
             q = qall[pl.ds(pl.multiple_of(first * rows, SUB * rows), SUB * rows), :]
@@ -216,6 +221,9 @@
                 s[h // 2] = lax.dot_general(
                     q, p_ref[h * LANES:(h + 2) * LANES, :],
                     (((1,), (1,)), ((), ())), preferred_element_type=f32)
+            if fetching:
+                find(first)
+                hold(first)
             for h in range(tiles):
                 for i in range(SUB):
                     for j in range(group):
@@ -265,7 +273,15 @@
         arrived(t.position(z, 1 - t.c, t.y, t.x))
         for _, y, x in t.plane():
             arrived(t.position(z, 1 - t.c, y, x))
-        score(z)
+
+        @pl.when(i == 1)
+        def _():
+            score(z, True)
+
+        @pl.when(i != 1)
+        def _():
+            score(z, False)
+
         return carry
 
     lax.fori_loop(0, t.nz, one_plane, 0)
@@ -273,13 +289,13 @@
     def one_fetch(i, carry):
         fetch(lax.rem(t.z + i, t.nz))
 
-        @pl.when(i == 1)
+        @pl.when(i == 2)
         def _():
             weigh()
 
         return carry
 
-    lax.fori_loop(1, t.nz, one_fetch, 0)
+    lax.fori_loop(2, t.nz, one_fetch, 0)
 
     at_row = iota((rows, r8 * LANES), 1)
     pick = (iota((rows, r8 * LANES), 0) == at_row % LANES // k * r8 + at_row // LANES).astype(f32).astype(bf16)

time: 59.5 us -> 61.1 us (1.027)
  Pallas kernels: 55.2 us -> 56.8 us
    pallas_call x1, Pallas kernels: 55.2 us -> 56.8 us  [body(): pl.pallas_call(functools.partial(kernel, (ny, nz, nx), scale, cap), out_s...]
where the time goes in v7:
time: 61.1 us; the launch traced here: 60.8 us
  Pallas kernels  56.8 us (93%)
  between operations  2.46 us (4%)
  other arithmetic  1.54 us (3%)
    pallas_call x1, Pallas kernels, body(): pl.pallas_call(functools.partial(kernel, (ny, nz, nx), scale, cap), out_s...  56.8 us
    mul x1, other arithmetic, body(): return (mean[0, 0], grads * scale)  1.54 us

profile of v7, /device:TPU:0, one launch (start us, length us, event | category | flops | bytes accessed | tf_op | source)
XLA Modules:
  0.0 60.8 jit_solution(2161045167745225507)
XLA Ops:
  0.6 56.8 %retriever_step.1 = (f32[32,768]{1,0:T(8,128)}, f32[1,1]{1,0:T(1,128)}) custom-call(bf16[32,768]{1,0:T(8,128)(2,1)} %q_hbm.1, bf16[2048,768]{1,0:T(8,128)(2,1)} %p_hbm.1, s32[32,32]{1,0:T(8,128)} %id_hbm.1, f32[32,32]{1,0:T(8,128)} %reader_hbm.1), custom_call_target="tpu_custom_call" | custom-call | tf_op jit(solution)/shard_map/retriever_step/pallas_call | solution.py:431
  57.5 1.5 %broadcast_multiply_fusion = f32[32,768]{1,0:T(8,128)} fusion(f32[32,768]{1,0:T(8,128)} %get-tuple-element.5), kind=kLoop, calls=%fused_computation | loop fusion | flops 24576 | bytes 196608 | tf_op jit(solution)/shard_map/mul | solution.py:464
